TPU v7x, 32 devices: a whole 2x2x4 slice. The times are simulated.
32 devices in a mesh: dp: 16 (over z, y, core), tensor: 2 (over x).
Axes of the slice: x: 2, y: 2, z: 4, core: 2. Of those that a mesh axis runs over, the one named last changes fastest.
Arguments:
- inputs: float32 [16384, 768], P('dp'), may hold values from -6 to 6
- pair_lengths: int32 [32, 3], P('dp'), may hold values from 0 to 464, as said below
- first_norm_gain: float32 [768], replicated, may hold values from 0.1 to 1.9
- first_norm_bias: float32 [768], replicated, may hold values from -1.75 to 1.75
- w_qkv: bfloat16 [768, 3, 768], P(None, None, 'tensor'), may hold values from -0.3125 to 0.3125
- b_qv: float32 [2, 768], P(None, 'tensor'), may hold values from -3 to 3
- w_out: bfloat16 [768, 768], P('tensor'), may hold values from -0.875 to 0.875
- b_out: float32 [768], replicated, may hold values from -3 to 3
- second_norm_gain: float32 [768], replicated, may hold values from 0.1 to 1.9
- second_norm_bias: float32 [768], replicated, may hold values from -1.75 to 1.75
- w_up: bfloat16 [768, 3072], P(None, 'tensor'), may hold values from -0.21875 to 0.21875
- b_up: float32 [3072], P('tensor'), may hold values from -3 to 3
- w_down: bfloat16 [3072, 768], P('tensor'), may hold values from -0.109375 to 0.109375
- b_down: float32 [768], replicated, may hold values from -3 to 3
- cotangent: float32 [16384, 768], P('dp'), may hold values from -6 to 6
Outputs:
- output: float32 [16384, 768], P('dp')
- gradient_of_input: float32 [16384, 768], P('dp')
- first_norm_gain_gradient: float32 [768], replicated
- grad_ln1_bias: float32 [768], replicated
- grad_w_qkv: float32 [768, 3, 768], P(None, None, 'tensor')
- grad_b_qv: float32 [2, 768], P(None, 'tensor')
- grad_w_out: float32 [768, 768], P('tensor')
- grad_b_out: float32 [768], replicated
- second_norm_gain_gradient: float32 [768], replicated
- grad_ln2_bias: float32 [768], replicated
- grad_w_up: float32 [768, 3072], P(None, 'tensor')
- grad_b_up: float32 [3072], P('tensor')
- grad_w_down: float32 [3072, 768], P('tensor')
- grad_b_down: float32 [768], replicated
Inputs may be any that keep to these rules, and one draw needn't show every extreme that they name: `pair_lengths`: each row lists the rows of the image-text pairs packed into one sequence in order: two or three pairs of 48 rows or more, a 0 in the last column where there is no third pair; a row sums to at most 512, the rest of the sequence is padding.
All inputs are finite; a program needn't handle non-finite values.
Results may differ from a plain program's by a relative error of at most 0.012.
The roundings to bfloat16 on the way count: a program that leaves them out, or rounds other values in their place, can miss the bound.
Values sent between devices are 32-bit elements; how exact they have to be, the bound alone decides.
No kernel may reach another device: no remote copies, remote signals or barrier semaphores. Data moves between devices by JAX's collectives and lax.ppermute only.
A program may use at most 192 MiB of HBM per device.

v0:
```python
import math

import jax
import jax.numpy as jnp
from jax import lax
from jax.sharding import PartitionSpec as P

HEAD_DIM = 64


EPS = 1e-06


def apply_layer_norm(values):
    row_mean = jnp.mean(values, -1, keepdims=True)
    centred = values - row_mean
    inverse_deviation = lax.rsqrt(jnp.mean(centred * centred, -1, keepdims=True) + EPS)
    return (centred * inverse_deviation, inverse_deviation)


def norm_backward_pass(
    normalized_gradient, norm_gain_factor, standardized_input, inverse_deviation
):
    scaled_rows = normalized_gradient * norm_gain_factor
    return inverse_deviation * (
        scaled_rows
        - jnp.mean(scaled_rows, -1, keepdims=True)
        - standardized_input * jnp.mean(scaled_rows * standardized_input, -1, keepdims=True)
    )


def segment_ids(pair_lengths, seq_len):
    pair_ends = jnp.cumsum(pair_lengths, axis=1)
    places = lax.broadcasted_iota(jnp.int32, (1, seq_len, 1), 1)
    return jnp.sum((places >= pair_ends[:, None, :]).astype(jnp.int32), axis=2)


def gelu_exact(values):
    return jax.nn.gelu(values, approximate=False)


def masked_scores(query_block, key_block, seg_block, scale_factor):
    raw_scores = (
        jnp.einsum("gqhd,gkhd->ghqk", query_block, key_block, preferred_element_type=jnp.float32)
        * scale_factor
    )
    same_seg = seg_block[:, None, :, None] == seg_block[:, None, None, :]
    return jnp.where(same_seg, raw_scores, -1e30)


def attend_forward(blocks, scale_factor):
    query_block, key_block, value_block, seg_block = blocks
    scores = masked_scores(query_block, key_block, seg_block, scale_factor)
    row_max = jnp.max(scores, -1, keepdims=True)
    exps = jnp.exp(scores - row_max)
    exp_total = jnp.sum(exps, -1, keepdims=True)
    weights = (exps / exp_total).astype(jnp.bfloat16)
    mixed = jnp.einsum("ghqk,gkhd->gqhd", weights, value_block, preferred_element_type=jnp.float32)
    return (mixed.astype(jnp.bfloat16), row_max + jnp.log(exp_total))


def attend_backward(blocks, scale_factor):
    query_block, key_block, value_block, seg_block, log_total, grad_mixed = blocks
    scores = masked_scores(query_block, key_block, seg_block, scale_factor)
    probs = jnp.exp(scores - log_total)
    probs_bf = probs.astype(jnp.bfloat16)
    grad_value = jnp.einsum(
        "ghqk,gqhd->gkhd", probs_bf, grad_mixed, preferred_element_type=jnp.float32
    )
    grad_probs = jnp.einsum(
        "gqhd,gkhd->ghqk", grad_mixed, value_block, preferred_element_type=jnp.float32
    )
    row_dot = jnp.sum(grad_probs * probs, -1, keepdims=True)
    grad_scores = (probs * (grad_probs - row_dot)).astype(jnp.bfloat16)
    grad_query = (
        jnp.einsum("ghqk,gkhd->gqhd", grad_scores, key_block, preferred_element_type=jnp.float32)
        * scale_factor
    )
    grad_key = (
        jnp.einsum("ghqk,gqhd->gkhd", grad_scores, query_block, preferred_element_type=jnp.float32)
        * scale_factor
    )
    return (grad_query, grad_key, grad_value)


def pack(arrays):
    return jnp.concatenate([piece.reshape(-1) for piece in arrays])


def unpack(flat, arrays):
    pieces = []
    offset = 0
    for piece in arrays:
        pieces.append(flat[offset : offset + piece.size].reshape(piece.shape))
        offset += piece.size
    return tuple(pieces)


def shards(
    inputs,
    pair_lengths,
    first_norm_gain,
    first_norm_bias,
    w_qkv,
    b_qv,
    w_out,
    b_out,
    second_norm_gain,
    second_norm_bias,
    w_up,
    b_up,
    w_down,
    b_down,
    cotangent,
):
    attn_shapes = (w_qkv, w_out, b_qv, b_out, first_norm_gain, first_norm_bias)
    mlp_shapes = (w_up, w_down, b_up, b_down, second_norm_gain, second_norm_bias)
    seq_count = pair_lengths.shape[0]
    token_count, width = inputs.shape
    seq_len = token_count // seq_count
    att_width = w_qkv.shape[2]
    head_count = att_width // HEAD_DIM
    scale_factor = 1.0 / math.sqrt(HEAD_DIM)
    per_group = math.gcd(seq_count, max(1, 512 // seq_len))
    group_count = seq_count // per_group
    seg_groups = segment_ids(pair_lengths, seq_len).reshape(group_count, per_group, seq_len)
    first_standardized, first_inverse_deviation = apply_layer_norm(inputs)
    normalized_rows = (first_standardized * first_norm_gain + first_norm_bias).astype(jnp.bfloat16)
    projected = jnp.dot(
        normalized_rows, w_qkv.reshape(width, 3 * att_width), preferred_element_type=jnp.float32
    )
    bias_rows = jnp.stack([b_qv[0], jnp.zeros_like(b_qv[0]), b_qv[1]])
    qkv_rows = (projected.reshape(token_count, 3, att_width) + bias_rows).astype(jnp.bfloat16)
    split_heads = qkv_rows.reshape(group_count, per_group, seq_len, 3, head_count, HEAD_DIM)
    query_all = split_heads[:, :, :, 0]
    key_all = split_heads[:, :, :, 1]
    value_all = split_heads[:, :, :, 2]

    def forward_block(blocks):
        return attend_forward(blocks, scale_factor)

    attended, log_totals = lax.map(forward_block, (query_all, key_all, value_all, seg_groups))
    attended = attended.reshape(token_count, att_width)
    branch = jnp.dot(attended, w_out, preferred_element_type=jnp.float32)
    branch_total = lax.all_gather(
        lax.psum_scatter(branch, "tensor", scatter_dimension=0, tiled=True),
        "tensor",
        axis=0,
        tiled=True,
    )
    residual_middle = inputs + branch_total + b_out
    second_standardized, second_inverse_deviation = apply_layer_norm(residual_middle)
    second_normalized_rows = (second_standardized * second_norm_gain + second_norm_bias).astype(
        jnp.bfloat16
    )
    pre_act = jnp.dot(second_normalized_rows, w_up, preferred_element_type=jnp.float32) + b_up
    activated, gelu_pull = jax.vjp(gelu_exact, pre_act)
    hidden_bf = activated.astype(jnp.bfloat16)
    down_part = jnp.dot(hidden_bf, w_down, preferred_element_type=jnp.float32)
    down_total = lax.all_gather(
        lax.psum_scatter(down_part, "tensor", scatter_dimension=0, tiled=True),
        "tensor",
        axis=0,
        tiled=True,
    )
    output = residual_middle + down_total + b_down
    out_bf = cotangent.astype(jnp.bfloat16)
    grad_b_down = jnp.sum(cotangent, 0)
    grad_w_down = jnp.einsum("tf,td->fd", hidden_bf, out_bf, preferred_element_type=jnp.float32)
    grad_hidden = jnp.einsum("td,fd->tf", out_bf, w_down, preferred_element_type=jnp.float32)
    grad_pre = gelu_pull(grad_hidden)[0].astype(jnp.bfloat16)
    grad_b_up = jnp.sum(grad_pre, 0, dtype=jnp.float32)
    grad_w_up = jnp.einsum(
        "td,tf->df", second_normalized_rows, grad_pre, preferred_element_type=jnp.float32
    )
    entry_two = jnp.einsum("tf,df->td", grad_pre, w_up, preferred_element_type=jnp.float32)
    second_normalized_gradient = lax.all_gather(
        lax.psum_scatter(entry_two, "tensor", scatter_dimension=0, tiled=True),
        "tensor",
        axis=0,
        tiled=True,
    )
    second_norm_gain_gradient = jnp.sum(second_normalized_gradient * second_standardized, 0)
    grad_ln2_bias = jnp.sum(second_normalized_gradient, 0)
    middle_state_gradient = cotangent + norm_backward_pass(
        second_normalized_gradient, second_norm_gain, second_standardized, second_inverse_deviation
    )
    mlp_flat = pack(
        (grad_w_up, grad_w_down, grad_b_up, grad_b_down, second_norm_gain_gradient, grad_ln2_bias)
    )
    mlp_part = lax.psum_scatter(mlp_flat, "dp", scatter_dimension=0, tiled=True)
    mlp_total = lax.all_gather(mlp_part, "dp", axis=0, tiled=True)
    grad_b_out = jnp.sum(middle_state_gradient, 0)
    middle_bf = middle_state_gradient.astype(jnp.bfloat16)
    grad_w_out = jnp.einsum("ta,td->ad", attended, middle_bf, preferred_element_type=jnp.float32)
    grad_attended = jnp.einsum(
        "td,ad->ta", middle_bf, w_out, preferred_element_type=jnp.float32
    ).astype(jnp.bfloat16)
    grad_heads = grad_attended.reshape(group_count, per_group, seq_len, head_count, HEAD_DIM)

    def backward_block(blocks):
        return attend_backward(blocks, scale_factor)

    grad_query, grad_key, grad_value = lax.map(
        backward_block, (query_all, key_all, value_all, seg_groups, log_totals, grad_heads)
    )
    grad_qkv = (
        jnp.stack([grad_query, grad_key, grad_value], axis=3)
        .reshape(token_count, 3, att_width)
        .astype(jnp.bfloat16)
    )
    grad_b_qv = jnp.stack(
        [
            jnp.sum(grad_qkv[:, 0], 0, dtype=jnp.float32),
            jnp.sum(grad_qkv[:, 2], 0, dtype=jnp.float32),
        ]
    )
    grad_w_qkv = jnp.einsum(
        "td,tca->dca", normalized_rows, grad_qkv, preferred_element_type=jnp.float32
    )
    entry_one = jnp.einsum("tca,dca->td", grad_qkv, w_qkv, preferred_element_type=jnp.float32)
    normalized_gradient = lax.all_gather(
        lax.psum_scatter(entry_one, "tensor", scatter_dimension=0, tiled=True),
        "tensor",
        axis=0,
        tiled=True,
    )
    first_norm_gain_gradient = jnp.sum(normalized_gradient * first_standardized, 0)
    grad_ln1_bias = jnp.sum(normalized_gradient, 0)
    gradient_of_input = middle_state_gradient + norm_backward_pass(
        normalized_gradient, first_norm_gain, first_standardized, first_inverse_deviation
    )
    attn_flat = pack(
        (grad_w_qkv, grad_w_out, grad_b_qv, grad_b_out, first_norm_gain_gradient, grad_ln1_bias)
    )
    attn_part = lax.psum_scatter(attn_flat, "dp", scatter_dimension=0, tiled=True)
    attn_summed = unpack(lax.all_gather(attn_part, "dp", axis=0, tiled=True), attn_shapes)
    mlp_summed = unpack(mlp_total, mlp_shapes)
    return (
        output,
        gradient_of_input,
        attn_summed[4],
        attn_summed[5],
        attn_summed[0],
        attn_summed[2],
        attn_summed[1],
        attn_summed[3],
        mlp_summed[4],
        mlp_summed[5],
        mlp_summed[0],
        mlp_summed[2],
        mlp_summed[1],
        mlp_summed[3],
    )


def solution(mesh):
    placed = (
        P("dp", None),
        P("dp", None),
        P(),
        P(),
        P(None, None, "tensor"),
        P(None, "tensor"),
        P("tensor", None),
        P(),
        P(),
        P(),
        P(None, "tensor"),
        P("tensor"),
        P("tensor", None),
        P(),
        P("dp", None),
    )
    return jax.shard_map(
        shards,
        mesh=mesh,
        in_specs=placed,
        out_specs=(
            P("dp", None),
            P("dp", None),
            P(),
            P(),
            P(None, None, "tensor"),
            P(None, "tensor"),
            P("tensor", None),
            P(),
            P(),
            P(),
            P(None, "tensor"),
            P("tensor"),
            P("tensor", None),
            P(),
        ),
        check_vma=False,
    )
```

profile of v0, /device:TPU:1, one launch (start us, length us, event | category | flops | bytes accessed | tf_op | source)
XLA Modules:
  0.0 1104.4 jit_solution(5125446046833521165)
XLA Ops:
  8.1 3.9 copy.93
  12.0 2.1 reduce_sum.180
  14.1 2.4 multiply_reduce_fusion.6
  16.7 6.3 add_convert_fusion.1
  22.9 4.3 copy.94
  27.2 6.6 reshape.350
  33.8 3.8 slice_bitcast_fusion
  40.2 2.1 copy.99
  42.3 13.6 %while.26 = (s32[]{:T(128)}, bf16[2,1,512,6,64]{2,4,3,1,0:T(8,128)(2,1)}, f32[2,1,6,512,1]{3,2,4,1,0:T(8,128)S(1)}, bf16[2,1,512,6,64]{2,4,3,1,0:T(8,128)(2,1)},...) while((s32[]{:T(128)}, ...), condition=%wide.region_7.8_spmd, body=%wide.region_4.7_spmd.sunk | while | flops 421983232 | bytes 31060152 | solution.py:142
  42.5 2.2 fusion.122
  49.1 2.2 fusion.122
  58.9 3.7 fusion.87
  62.7 45.5 %reduce-scatter.5.cloned.1.call-done = f32[512,768]{1,0:T(8,128)} async-done(((f32[1024,768]{1,0:T(8,128)}), f32[512,768]{1,0:T(8,128)}) %reduce-scatter.5.cloned.1.call-update) | async-done | bytes 1572880 | tf_op jit(solution)/shard_map/reduce_scatter | solution.py:146
  108.3 46.5 %all-gather.5.cloned.1.call-done = f32[1024,768]{1,0:T(8,128)} async-done(((f32[512,768]{1,0:T(8,128)}), f32[1024,768]{1,0:T(8,128)}) %all-gather.5.cloned.1.call-update) | async-done | bytes 3145744 | tf_op jit(solution)/shard_map/all_gather | solution.py:145
  154.8 3.3 fusion.81
  158.7 17.5 %multiply_convert_fusion.1 = (bf16[1024,1536]{1,0:T(8,128)(2,1)}, f32[1024,1536]{1,0:T(8,128)S(1)}, f32[1024,1536]{1,0:T(8,128)}) fusion(f32[1536]{0:T(1024)S(1)} %copy-done.37, bf16[768,1536]{1,0:T(8,128)(2,1)S(1)} %copy-done, f32[1024,768]{1,0:T(8,128)S(1)} %get-tuple-element.265, f32[768]{0:T(1024)S(1)} %copy-done.38, f32[768]{0:T(1024)S(1)} %copy-done.29, ...), kind=kOutput, calls=%fused_computation.67 | convolution fusion | flops 2523660288 | bytes 21254144 | tf_op jit(solution)/shard_map/dot_general | solution.py:156
  176.2 6.7 convert_reduce_fusion
  184.6 4.3 fusion.89
  188.9 7.0 fusion.88
  196.1 8.2 fusion.77
  204.3 5.6 reshape.358
  209.9 22.5 %reduce-scatter.9.cloned.1.call-done = f32[512,768]{1,0:T(8,128)} async-done(((f32[1024,768]{1,0:T(8,128)}), f32[512,768]{1,0:T(8,128)}) %reduce-scatter.9.cloned.1.call-update) | async-done | bytes 1572880 | tf_op jit(solution)/shard_map/reduce_scatter | solution.py:178
  232.5 4.4 constant_dynamic-update-slice_fusion.3
  238.4 4.4 fusion.66
  242.8 5.7 reshape.359
  248.5 29.4 %reduce-scatter.7.cloned.1.call-done = f32[512,768]{1,0:T(8,128)} async-done(((f32[1024,768]{1,0:T(8,128)}), f32[512,768]{1,0:T(8,128)}) %reduce-scatter.7.cloned.1.call-update) | async-done | bytes 1572880 | tf_op jit(solution)/shard_map/reduce_scatter | solution.py:161
  278.1 4.0 constant_dynamic-update-slice_fusion.1
  283.4 40.9 %all-gather.9.cloned.1.call-done = f32[1024,768]{1,0:T(8,128)} async-done(((f32[512,768]{1,0:T(8,128)}), f32[1024,768]{1,0:T(8,128)}) %all-gather.9.cloned.1.call-update) | async-done | bytes 3145744 | tf_op jit(solution)/shard_map/all_gather | solution.py:177
  324.3 3.6 multiply_reduce_fusion.1
  327.9 42.8 %all-gather.7.cloned.1.call-done = f32[1024,768]{1,0:T(8,128)} async-done(((f32[512,768]{1,0:T(8,128)}), f32[1024,768]{1,0:T(8,128)}) %all-gather.7.cloned.1.call-update) | async-done | bytes 3145744 | tf_op jit(solution)/shard_map/all_gather | solution.py:160
  370.8 7.3 fusion.79
  378.0 2.9 convolution_convert_fusion
  382.8 27.5 %while.27 = (s32[]{:T(128)}, bf16[2,1,512,6,64]{2,4,3,1,0:T(8,128)(2,1)}, bf16[2,1,512,6,64]{2,4,3,1,0:T(8,128)(2,1)}, bf16[2,1,512,6,64]{2,4,3,1,0:T(8,128)(2,1...) while((s32[]{:T(128)}, ...), condition=%wide.region_17.18_spmd, body=%wide.region_15.17_spmd.sunk | while | flops 1030878208 | bytes 69180680 | solution.py:204
  382.8 2.1 fusion.133
  385.2 2.2 multiply_reduce_fusion.10
  389.4 2.5 fusion.134
  396.4 2.1 fusion.133
  398.8 2.2 multiply_reduce_fusion.10
  403.1 2.5 fusion.134
  420.1 6.3 convolution_bitcast_fusion
  426.4 6.0 fusion.62
  432.4 3.8 fusion.63
  436.9 6.7 copy.114
  443.6 6.6 reshape.354
  450.3 2.3 reshape.355
  452.6 4.1 constant_dynamic-update-slice_fusion.2
  456.7 23.4 %reduce-scatter.11.cloned.1.call-done = f32[512,768]{1,0:T(8,128)} async-done(((f32[1024,768]{1,0:T(8,128)}), f32[512,768]{1,0:T(8,128)}) %reduce-scatter.11.cloned.1.call-update) | async-done | bytes 1572880 | tf_op jit(solution)/shard_map/reduce_scatter | solution.py:223
  480.2 2.4 constant_dynamic-update-slice_fusion.7
  488.3 38.3 %all-gather.11.cloned.1.call-done = f32[1024,768]{1,0:T(8,128)} async-done(((f32[512,768]{1,0:T(8,128)}), f32[1024,768]{1,0:T(8,128)}) %all-gather.11.cloned.1.call-update) | async-done | bytes 3145744 | tf_op jit(solution)/shard_map/all_gather | solution.py:222
  526.6 3.0 multiply_reduce_fusion.2
  536.0 256.4 %all-reduce.11.cloned.1.call-done = (f32[1182720]{0:T(1024)}, f32[2363136]{0:T(1024)}) async-done(((f32[1182720]{0:T(1024)}, f32[2363136]{0:T(1024)}), (f32[1182720]{0:T(1024)}, f32[2363136]{0:T(1024)})) %all-reduce.11.cloned.1.call-update) | async-done | bytes 14183440
  792.4 2.4 broadcast.169
  794.8 2.1 dynamic-slice_dynamic-update-slice_fusion.1
  796.9 3.9 broadcast.170
  800.8 2.6 dynamic-slice_dynamic-update-slice_fusion
  803.4 4.5 multiply_add_fusion
  807.9 254.9 %all-reduce.9.cloned.1.call-done = (f32[1182720]{0:T(1024)}, f32[2363136]{0:T(1024)}) async-done(((f32[1182720]{0:T(1024)}, f32[2363136]{0:T(1024)}), (f32[1182720]{0:T(1024)}, f32[2363136]{0:T(1024)})) %all-reduce.9.cloned.1.call-update) | async-done | bytes 14183440
  1064.2 2.4 slice.108
  1066.6 2.7 slice.110
  1070.6 3.9 fusion.83
  1075.2 3.7 reshape.357
  1078.9 4.5 copy.115
  1085.2 5.8 reshape.360
  1091.0 6.1 slice.101
  (200 shorter events, 61.6 us)
Async XLA Ops:
  7.2 151.4 %copy-start = (bf16[768,1536]{1,0:T(8,128)(2,1)S(1)}, bf16[768,1536]{1,0:T(8,128)(2,1)}, u32[]{:S(2)}) copy-start(bf16[768,1536]{1,0:T(8,128)(2,1)} %param.29) | copy-start | bytes 7077892
  7.2 101.0 %reduce-scatter.5.cloned.1.call-start = ((), (), s32[]{:S(2)}) async-start(), calls=%async_computation.4 | async-start | bytes 4718592 | tf_op jit(solution)/shard_map/reduce_scatter | solution.py:146
  8.1 8.5 copy-start.30
  8.1 8.5 copy-start.39
  14.1 8.8 copy-start.25
  16.5 6.4 copy-start.27
  27.2 11.4 %copy-start.35 = (s32[2,3]{1,0:T(2,128)S(1)}, s32[2,3]{1,0:T(2,128)}, u32[]{:S(2)}) copy-start(s32[2,3]{1,0:T(2,128)} %param.20) | copy-start | bytes 76
  44.7 1.3 copy-start.4
  44.7 1.4 copy-start.23
  48.0 0.9 copy-start.24
  51.3 1.3 copy-start.4
  51.3 1.4 copy-start.23
  54.7 0.9 copy-start.24
  58.0 0.9 copy-start.13
  58.0 96.8 %copy-start.32 = (f32[768]{0:T(1024)S(1)}, f32[768]{0:T(1024)}, u32[]{:S(2)}) copy-start(f32[768]{0:T(1024)} %param.26) | copy-start | bytes 9220
  62.6 92.2 %all-gather.5.cloned.1.call-start = ((), (), s32[]{:S(2)}) async-start(), calls=%async_computation.5 | async-start | bytes 4718592 | tf_op jit(solution)/shard_map/all_gather | solution.py:145
  108.2 50.4 %copy-start.29 = (f32[768]{0:T(1024)S(1)}, f32[768]{0:T(1024)}, u32[]{:S(2)}) copy-start(f32[768]{0:T(1024)} %param.27) | copy-start | bytes 9220
  108.2 50.4 %copy-start.37 = (f32[1536]{0:T(1024)S(1)}, f32[1536]{0:T(1024)}, u32[]{:S(2)}) copy-start(f32[1536]{0:T(1024)} %param.30) | copy-start | bytes 18436
  108.2 50.4 %copy-start.38 = (f32[768]{0:T(1024)S(1)}, f32[768]{0:T(1024)}, u32[]{:S(2)}) copy-start(f32[768]{0:T(1024)} %param.28) | copy-start | bytes 9220
  108.3 124.1 %reduce-scatter.9.cloned.1.call-start = ((), (), s32[]{:S(2)}) async-start(), calls=%async_computation.8 | async-start | bytes 4718592 | tf_op jit(solution)/shard_map/reduce_scatter | solution.py:178
  158.1 18.1 %copy-start.3 = (f32[1024,768]{1,0:T(8,128)}, f32[1024,768]{1,0:T(8,128)S(1)}, u32[]{:S(2)}) copy-start(f32[1024,768]{1,0:T(8,128)S(1)} %get-tuple-element.265) | copy-start | bytes 9437188
  158.7 17.5 %copy-start.16 = (f32[1024,768]{1,0:T(8,128)S(1)}, f32[1024,768]{1,0:T(8,128)}, u32[]{:S(2)}) copy-start(f32[1024,768]{1,0:T(8,128)} %param.33) | copy-start | bytes 9437188
  158.7 17.5 %copy-start.36 = (bf16[1536,768]{1,0:T(8,128)(2,1)S(1)}, bf16[1536,768]{1,0:T(8,128)(2,1)}, u32[]{:S(2)}) copy-start(bf16[1536,768]{1,0:T(8,128)(2,1)} %param.31) | copy-start | bytes 7077892
  182.9 1.7 copy-start.42
  188.9 89.0 %reduce-scatter.7.cloned.1.call-start = ((), (), s32[]{:S(2)}) async-start(), calls=%async_computation.6 | async-start | bytes 4718592 | tf_op jit(solution)/shard_map/reduce_scatter | solution.py:161
  196.0 128.3 %all-gather.9.cloned.1.call-start = ((), (), s32[]{:S(2)}) async-start(), calls=%async_computation.9 | async-start | bytes 4718592 | tf_op jit(solution)/shard_map/all_gather | solution.py:177
  232.4 138.3 %all-gather.7.cloned.1.call-start = ((), (), s32[]{:S(2)}) async-start(), calls=%async_computation.7 | async-start | bytes 4718592 | tf_op jit(solution)/shard_map/all_gather | solution.py:160
  232.5 4.4 copy-start.17
  232.5 6.0 copy-start.41
  277.9 202.2 %reduce-scatter.11.cloned.1.call-start = ((), (), s32[]{:S(2)}) async-start(), calls=%async_computation.10 | async-start | bytes 4718592 | tf_op jit(solution)/shard_map/reduce_scatter | solution.py:223
  282.1 88.7 %copy-start.33 = (f32[768]{0:T(1024)S(1)}, f32[768]{0:T(1024)}, u32[]{:S(2)}) copy-start(f32[768]{0:T(1024)} %param.32) | copy-start | bytes 9220
  370.8 7.3 copy-start.18
  382.8 2.4 copy-start.5
  382.8 2.4 copy-start.6
  389.4 4.4 copy-start.7
  389.4 4.3 copy-start.21
  395.5 0.9 copy-start.22
  396.4 2.4 copy-start.5
  396.4 2.4 copy-start.6
  403.0 4.3 copy-start.7
  403.0 4.3 copy-start.21
  409.1 0.9 copy-start.22
  410.3 3.8 copy-start.20
  410.3 6.4 copy-start.19
  412.9 5.1 copy-start.9
  418.1 0.9 copy-start.11
  420.1 6.3 copy-start.2
  420.1 6.3 copy-start.26
  420.1 6.3 copy-start.28
  420.1 6.3 copy-start.31
  420.1 6.3 copy-start.40
  426.4 6.0 copy-start.14
  432.4 3.8 copy-start.10
  432.4 4.0 copy-start.12
  436.6 90.0 %all-gather.11.cloned.1.call-start = ((), (), s32[]{:S(2)}) async-start(), calls=%async_computation.11 | async-start | bytes 4718592 | tf_op jit(solution)/shard_map/all_gather | solution.py:222
  480.1 312.3 %all-reduce.11.cloned.1.call-start = ((), (), s32[]{:S(2)}) async-start(), calls=%async_computation.13 | async-start | bytes 28368896
  532.2 0.7 copy-start.34
  532.2 530.6 %all-reduce.9.cloned.1.call-start = ((), (), s32[]{:S(2)}) async-start(), calls=%async_computation.12 | async-start | bytes 28368896
  1064.2 6.4 copy-start.8
  1078.9 5.0 copy-start.15
  1091.0 6.1 copy-start.1
Sparse Core Ops, SparseCore 0:
  62.7 45.4 reduce-scatter.4
  109.8 44.9 all-gather.4
  189.0 43.3 reduce-scatter.8
  234.5 43.3 reduce-scatter.6
  279.3 44.9 all-gather.8
  325.8 44.9 all-gather.6
  436.7 43.3 reduce-scatter.10
  481.7 44.9 all-gather.10
  532.3 260.0 all-reduce.10
  803.5 259.2 all-reduce.8
where the time goes:
time: 1110 us; the launch traced here: 1100 us
  waiting for transfers between devices  801 us (72%)
  local copies, waits for them, and re-layouts  143 us (13%)
  matrix products  106 us (10%)
  other arithmetic  34.7 us (3%)
  between operations  17.7 us (2%)
    unnamed x12, waiting for transfers between devices  511 us
    unnamed x88, local copies, waits for them, and re-layouts  48.2 us
    all_gather x1, waiting for transfers between devices, shards(): lax.all_gather(lax.psum_scatter(branch, 'tensor', scatter_dimension=0, ti...  46.5 us
    reduce_scatter x1, waiting for transfers between devices, shards(): lax.psum_scatter(branch, 'tensor', scatter_dimension=0, tiled=True)  45.5 us
    all_gather x1, waiting for transfers between devices, shards(): lax.all_gather(lax.psum_scatter(down_part, 'tensor', scatter_dimension=0,...  42.8 us
    all_gather x1, waiting for transfers between devices, shards(): lax.all_gather(lax.psum_scatter(entry_two, 'tensor', scatter_dimension=0,...  40.9 us
    all_gather x1, waiting for transfers between devices, shards(): lax.all_gather(lax.psum_scatter(entry_one, 'tensor', scatter_dimension=0,...  38.3 us
    reduce_scatter x1, waiting for transfers between devices, shards(): lax.psum_scatter(down_part, 'tensor', scatter_dimension=0, tiled=True)  29.4 us
  transfers between devices with their start and end apart: 10, of which 10 were waited for; matrix products, arithmetic and copies ran while one was open for 7% of the time, Pallas kernels for 0%

commit v1 on v0

--- a/solution.py
+++ b/solution.py
@@ -30,7 +30,9 @@
 
 
 def segment_ids(pair_lengths, seq_len):
-    pair_ends = jnp.cumsum(pair_lengths, axis=1)
+    first_end = pair_lengths[:, 0]
+    second_end = first_end + pair_lengths[:, 1]
+    pair_ends = jnp.stack([first_end, second_end, second_end + pair_lengths[:, 2]], axis=1)
     places = lax.broadcasted_iota(jnp.int32, (1, seq_len, 1), 1)
     return jnp.sum((places >= pair_ends[:, None, :]).astype(jnp.int32), axis=2)
 

time: 1110 us -> 1110 us (level)
  no operation moved by 1% of the time
where the time goes in v1:
time: 1110 us; the launch traced here: 1100 us
  waiting for transfers between devices  801 us (72%)
  local copies, waits for them, and re-layouts  143 us (13%)
  matrix products  106 us (10%)
  other arithmetic  34.7 us (3%)
  between operations  17.7 us (2%)
    unnamed x12, waiting for transfers between devices  511 us
    unnamed x88, local copies, waits for them, and re-layouts  48.3 us
    all_gather x1, waiting for transfers between devices, shards(): lax.all_gather(lax.psum_scatter(branch, 'tensor', scatter_dimension=0, ti...  46.5 us
    reduce_scatter x1, waiting for transfers between devices, shards(): lax.psum_scatter(branch, 'tensor', scatter_dimension=0, tiled=True)  45.5 us
    all_gather x1, waiting for transfers between devices, shards(): lax.all_gather(lax.psum_scatter(down_part, 'tensor', scatter_dimension=0,...  42.8 us
    all_gather x1, waiting for transfers between devices, shards(): lax.all_gather(lax.psum_scatter(entry_two, 'tensor', scatter_dimension=0,...  40.9 us
    all_gather x1, waiting for transfers between devices, shards(): lax.all_gather(lax.psum_scatter(entry_one, 'tensor', scatter_dimension=0,...  38.3 us
    reduce_scatter x1, waiting for transfers between devices, shards(): lax.psum_scatter(down_part, 'tensor', scatter_dimension=0, tiled=True)  29.4 us
  transfers between devices with their start and end apart: 10, of which 10 were waited for; matrix products, arithmetic and copies ran while one was open for 7% of the time, Pallas kernels for 0%

profile of v1, /device:TPU:1, one launch (start us, length us, event | category | flops | bytes accessed | tf_op | source)
XLA Modules:
  0.0 1104.4 jit_solution(241988513625199068)
XLA Ops:
  8.1 3.9 copy.93
  12.0 2.1 reduce_sum.180
  14.1 2.4 multiply_reduce_fusion.6
  16.7 6.3 add_convert_fusion.1
  22.9 4.3 copy.94
  27.2 6.6 reshape.348
  33.8 3.8 slice_bitcast_fusion
  40.1 2.1 copy.99
  42.2 13.6 %while.26 = (s32[]{:T(128)}, bf16[2,1,512,6,64]{2,4,3,1,0:T(8,128)(2,1)}, f32[2,1,6,512,1]{3,2,4,1,0:T(8,128)S(1)}, bf16[2,1,512,6,64]{2,4,3,1,0:T(8,128)(2,1)},...) while((s32[]{:T(128)}, ...), condition=%wide.region_6.7_spmd, body=%wide.region_3.6_spmd.sunk | while | flops 421983232 | bytes 31060152 | solution.py:144
  42.5 2.2 fusion.122
  49.1 2.2 fusion.122
  58.8 3.7 fusion.87
  62.7 45.5 %reduce-scatter.5.cloned.1.call-done = f32[512,768]{1,0:T(8,128)} async-done(((f32[1024,768]{1,0:T(8,128)}), f32[512,768]{1,0:T(8,128)}) %reduce-scatter.5.cloned.1.call-update) | async-done | bytes 1572880 | tf_op jit(solution)/shard_map/reduce_scatter | solution.py:148
  108.3 46.5 %all-gather.5.cloned.1.call-done = f32[1024,768]{1,0:T(8,128)} async-done(((f32[512,768]{1,0:T(8,128)}), f32[1024,768]{1,0:T(8,128)}) %all-gather.5.cloned.1.call-update) | async-done | bytes 3145744 | tf_op jit(solution)/shard_map/all_gather | solution.py:147
  154.8 3.3 fusion.81
  158.7 17.5 %multiply_convert_fusion.1 = (bf16[1024,1536]{1,0:T(8,128)(2,1)}, f32[1024,1536]{1,0:T(8,128)S(1)}, f32[1024,1536]{1,0:T(8,128)}) fusion(f32[1536]{0:T(1024)S(1)} %copy-done.37, bf16[768,1536]{1,0:T(8,128)(2,1)S(1)} %copy-done, f32[1024,768]{1,0:T(8,128)S(1)} %get-tuple-element.265, f32[768]{0:T(1024)S(1)} %copy-done.38, f32[768]{0:T(1024)S(1)} %copy-done.29, ...), kind=kOutput, calls=%fused_computation.67 | convolution fusion | flops 2523660288 | bytes 21254144 | tf_op jit(solution)/shard_map/dot_general | solution.py:158
  176.2 6.7 convert_reduce_fusion
  184.5 4.3 fusion.89
  188.9 7.0 fusion.88
  196.1 8.2 fusion.77
  204.3 5.6 reshape.356
  209.9 22.5 %reduce-scatter.9.cloned.1.call-done = f32[512,768]{1,0:T(8,128)} async-done(((f32[1024,768]{1,0:T(8,128)}), f32[512,768]{1,0:T(8,128)}) %reduce-scatter.9.cloned.1.call-update) | async-done | bytes 1572880 | tf_op jit(solution)/shard_map/reduce_scatter | solution.py:180
  232.5 4.4 constant_dynamic-update-slice_fusion.3
  238.4 4.4 fusion.66
  242.8 5.7 reshape.357
  248.5 29.4 %reduce-scatter.7.cloned.1.call-done = f32[512,768]{1,0:T(8,128)} async-done(((f32[1024,768]{1,0:T(8,128)}), f32[512,768]{1,0:T(8,128)}) %reduce-scatter.7.cloned.1.call-update) | async-done | bytes 1572880 | tf_op jit(solution)/shard_map/reduce_scatter | solution.py:163
  278.1 3.9 constant_dynamic-update-slice_fusion.1
  283.4 40.9 %all-gather.9.cloned.1.call-done = f32[1024,768]{1,0:T(8,128)} async-done(((f32[512,768]{1,0:T(8,128)}), f32[1024,768]{1,0:T(8,128)}) %all-gather.9.cloned.1.call-update) | async-done | bytes 3145744 | tf_op jit(solution)/shard_map/all_gather | solution.py:179
  324.3 3.6 multiply_reduce_fusion.1
  327.9 42.8 %all-gather.7.cloned.1.call-done = f32[1024,768]{1,0:T(8,128)} async-done(((f32[512,768]{1,0:T(8,128)}), f32[1024,768]{1,0:T(8,128)}) %all-gather.7.cloned.1.call-update) | async-done | bytes 3145744 | tf_op jit(solution)/shard_map/all_gather | solution.py:162
  370.7 7.3 fusion.79
  378.0 2.9 convolution_convert_fusion
  382.7 27.5 %while.27 = (s32[]{:T(128)}, bf16[2,1,512,6,64]{2,4,3,1,0:T(8,128)(2,1)}, bf16[2,1,512,6,64]{2,4,3,1,0:T(8,128)(2,1)}, bf16[2,1,512,6,64]{2,4,3,1,0:T(8,128)(2,1...) while((s32[]{:T(128)}, ...), condition=%wide.region_16.17_spmd, body=%wide.region_14.16_spmd.sunk | while | flops 1030878208 | bytes 69180680 | solution.py:206
  382.7 2.1 fusion.133
  385.2 2.2 multiply_reduce_fusion.10
  389.4 2.5 fusion.134
  396.4 2.1 fusion.133
  398.8 2.2 multiply_reduce_fusion.10
  403.0 2.5 fusion.134
  420.2 6.3 convolution_bitcast_fusion
  426.4 6.0 fusion.62
  432.4 3.8 fusion.63
  437.0 6.7 copy.114
  443.7 6.6 reshape.352
  450.3 2.3 reshape.353
  452.7 4.1 constant_dynamic-update-slice_fusion.2
  456.7 23.4 %reduce-scatter.11.cloned.1.call-done = f32[512,768]{1,0:T(8,128)} async-done(((f32[1024,768]{1,0:T(8,128)}), f32[512,768]{1,0:T(8,128)}) %reduce-scatter.11.cloned.1.call-update) | async-done | bytes 1572880 | tf_op jit(solution)/shard_map/reduce_scatter | solution.py:225
  480.2 2.4 constant_dynamic-update-slice_fusion.7
  488.4 38.3 %all-gather.11.cloned.1.call-done = f32[1024,768]{1,0:T(8,128)} async-done(((f32[512,768]{1,0:T(8,128)}), f32[1024,768]{1,0:T(8,128)}) %all-gather.11.cloned.1.call-update) | async-done | bytes 3145744 | tf_op jit(solution)/shard_map/all_gather | solution.py:224
  526.7 3.0 multiply_reduce_fusion.2
  536.0 256.4 %all-reduce.11.cloned.1.call-done = (f32[1182720]{0:T(1024)}, f32[2363136]{0:T(1024)}) async-done(((f32[1182720]{0:T(1024)}, f32[2363136]{0:T(1024)}), (f32[1182720]{0:T(1024)}, f32[2363136]{0:T(1024)})) %all-reduce.11.cloned.1.call-update) | async-done | bytes 14183440
  792.4 2.4 broadcast.170
  794.8 2.1 dynamic-slice_dynamic-update-slice_fusion.1
  796.9 3.9 broadcast.171
  800.8 2.6 dynamic-slice_dynamic-update-slice_fusion
  803.4 4.5 multiply_add_fusion
  807.9 254.9 %all-reduce.9.cloned.1.call-done = (f32[1182720]{0:T(1024)}, f32[2363136]{0:T(1024)}) async-done(((f32[1182720]{0:T(1024)}, f32[2363136]{0:T(1024)}), (f32[1182720]{0:T(1024)}, f32[2363136]{0:T(1024)})) %all-reduce.9.cloned.1.call-update) | async-done | bytes 14183440
  1064.2 2.4 slice.120
  1066.6 2.7 slice.122
  1070.7 4.0 fusion.83
  1075.2 3.7 reshape.355
  1078.9 4.5 copy.115
  1085.2 5.8 reshape.358
  1091.0 6.1 slice.113
  (201 shorter events, 61.7 us)
Async XLA Ops:
  7.2 151.4 %copy-start = (bf16[768,1536]{1,0:T(8,128)(2,1)S(1)}, bf16[768,1536]{1,0:T(8,128)(2,1)}, u32[]{:S(2)}) copy-start(bf16[768,1536]{1,0:T(8,128)(2,1)} %param.29) | copy-start | bytes 7077892
  7.2 101.0 %reduce-scatter.5.cloned.1.call-start = ((), (), s32[]{:S(2)}) async-start(), calls=%async_computation.4 | async-start | bytes 4718592 | tf_op jit(solution)/shard_map/reduce_scatter | solution.py:148
  8.1 8.5 copy-start.30
  8.1 8.5 copy-start.39
  14.1 8.8 copy-start.25
  16.5 6.4 copy-start.27
  27.2 11.4 %copy-start.32 = (s32[2,3]{1,0:T(2,128)S(1)}, s32[2,3]{1,0:T(2,128)}, u32[]{:S(2)}) copy-start(s32[2,3]{1,0:T(2,128)} %param.20) | copy-start | bytes 76
  44.7 1.3 copy-start.4
  44.7 1.4 copy-start.23
  48.0 0.9 copy-start.24
  51.3 1.3 copy-start.4
  51.3 1.4 copy-start.23
  54.6 0.9 copy-start.24
  57.9 0.9 copy-start.13
  57.9 96.8 %copy-start.33 = (f32[768]{0:T(1024)S(1)}, f32[768]{0:T(1024)}, u32[]{:S(2)}) copy-start(f32[768]{0:T(1024)} %param.26) | copy-start | bytes 9220
  62.6 92.2 %all-gather.5.cloned.1.call-start = ((), (), s32[]{:S(2)}) async-start(), calls=%async_computation.5 | async-start | bytes 4718592 | tf_op jit(solution)/shard_map/all_gather | solution.py:147
  108.2 50.4 %copy-start.29 = (f32[768]{0:T(1024)S(1)}, f32[768]{0:T(1024)}, u32[]{:S(2)}) copy-start(f32[768]{0:T(1024)} %param.27) | copy-start | bytes 9220
  108.2 50.4 %copy-start.37 = (f32[1536]{0:T(1024)S(1)}, f32[1536]{0:T(1024)}, u32[]{:S(2)}) copy-start(f32[1536]{0:T(1024)} %param.30) | copy-start | bytes 18436
  108.2 50.4 %copy-start.38 = (f32[768]{0:T(1024)S(1)}, f32[768]{0:T(1024)}, u32[]{:S(2)}) copy-start(f32[768]{0:T(1024)} %param.28) | copy-start | bytes 9220
  108.2 124.1 %reduce-scatter.9.cloned.1.call-start = ((), (), s32[]{:S(2)}) async-start(), calls=%async_computation.8 | async-start | bytes 4718592 | tf_op jit(solution)/shard_map/reduce_scatter | solution.py:180
  158.1 18.1 %copy-start.3 = (f32[1024,768]{1,0:T(8,128)}, f32[1024,768]{1,0:T(8,128)S(1)}, u32[]{:S(2)}) copy-start(f32[1024,768]{1,0:T(8,128)S(1)} %get-tuple-element.265) | copy-start | bytes 9437188
  158.6 17.5 %copy-start.16 = (f32[1024,768]{1,0:T(8,128)S(1)}, f32[1024,768]{1,0:T(8,128)}, u32[]{:S(2)}) copy-start(f32[1024,768]{1,0:T(8,128)} %param.33) | copy-start | bytes 9437188
  158.7 17.5 %copy-start.36 = (bf16[1536,768]{1,0:T(8,128)(2,1)S(1)}, bf16[1536,768]{1,0:T(8,128)(2,1)}, u32[]{:S(2)}) copy-start(bf16[1536,768]{1,0:T(8,128)(2,1)} %param.31) | copy-start | bytes 7077892
  182.9 1.7 copy-start.42
  188.9 89.0 %reduce-scatter.7.cloned.1.call-start = ((), (), s32[]{:S(2)}) async-start(), calls=%async_computation.6 | async-start | bytes 4718592 | tf_op jit(solution)/shard_map/reduce_scatter | solution.py:163
  196.0 128.3 %all-gather.9.cloned.1.call-start = ((), (), s32[]{:S(2)}) async-start(), calls=%async_computation.9 | async-start | bytes 4718592 | tf_op jit(solution)/shard_map/all_gather | solution.py:179
  232.4 138.3 %all-gather.7.cloned.1.call-start = ((), (), s32[]{:S(2)}) async-start(), calls=%async_computation.7 | async-start | bytes 4718592 | tf_op jit(solution)/shard_map/all_gather | solution.py:162
  232.4 4.4 copy-start.17
  232.5 6.0 copy-start.41
  277.9 202.3 %reduce-scatter.11.cloned.1.call-start = ((), (), s32[]{:S(2)}) async-start(), calls=%async_computation.10 | async-start | bytes 4718592 | tf_op jit(solution)/shard_map/reduce_scatter | solution.py:225
  282.1 88.7 %copy-start.34 = (f32[768]{0:T(1024)S(1)}, f32[768]{0:T(1024)}, u32[]{:S(2)}) copy-start(f32[768]{0:T(1024)} %param.32) | copy-start | bytes 9220
  370.7 7.3 copy-start.18
  382.7 2.4 copy-start.5
  382.7 2.4 copy-start.6
  389.3 4.4 copy-start.7
  389.3 4.3 copy-start.21
  395.5 0.9 copy-start.22
  396.4 2.4 copy-start.5
  396.4 2.4 copy-start.6
  403.0 4.4 copy-start.7
  403.0 4.4 copy-start.21
  409.1 0.9 copy-start.22
  410.3 3.8 copy-start.20
  410.3 6.4 copy-start.19
  412.9 5.1 copy-start.9
  418.1 0.9 copy-start.11
  420.1 6.3 copy-start.2
  420.1 6.3 copy-start.26
  420.1 6.3 copy-start.28
  420.1 6.3 copy-start.31
  420.1 6.3 copy-start.40
  426.4 6.0 copy-start.14
  432.4 3.8 copy-start.10
  432.4 4.0 copy-start.12
  436.7 90.0 %all-gather.11.cloned.1.call-start = ((), (), s32[]{:S(2)}) async-start(), calls=%async_computation.11 | async-start | bytes 4718592 | tf_op jit(solution)/shard_map/all_gather | solution.py:224
  480.2 312.2 %all-reduce.11.cloned.1.call-start = ((), (), s32[]{:S(2)}) async-start(), calls=%async_computation.13 | async-start | bytes 28368896
  532.2 0.7 copy-start.35
  532.2 530.6 %all-reduce.9.cloned.1.call-start = ((), (), s32[]{:S(2)}) async-start(), calls=%async_computation.12 | async-start | bytes 28368896
  1064.2 6.4 copy-start.8
  1078.9 5.0 copy-start.15
  1091.0 6.1 copy-start.1
Sparse Core Ops, SparseCore 0:
  62.7 45.4 reduce-scatter.4
  109.8 44.9 all-gather.4
  189.0 43.3 reduce-scatter.8
  234.5 43.3 reduce-scatter.6
  279.3 44.9 all-gather.8
  325.8 44.9 all-gather.6
  436.8 43.3 reduce-scatter.10
  481.7 44.9 all-gather.10
  532.4 260.0 all-reduce.10
  803.5 259.2 all-reduce.8

commit v2 on v0

v2 whole, which is shorter than its diff:
```python
import functools
import math

import jax
import jax.numpy as jnp
from jax import lax
from jax.experimental import pallas as pl
from jax.experimental.pallas import tpu as pltpu
from jax.sharding import PartitionSpec as P

HEAD_DIM = 64
LANES = 128
EPS = 1e-06
MASKED = -1e30
VMEM_BYTES = 56 * 1024 * 1024
F32 = jnp.float32
BF16 = jnp.bfloat16
ERFC_P = 0.3925
ERFC_C = (
    0.2342248384381894,
    0.1104885068031651,
    0.6008554065531575,
    -0.5658356357906557,
    0.8411781949001069,
    -0.22091131771921121,
)


def dot(left, right):
    return lax.dot_general(left, right, (((1,), (0,)), ((), ())), preferred_element_type=F32)


def dot_bt(left, right):
    return lax.dot_general(left, right, (((1,), (1,)), ((), ())), preferred_element_type=F32)


def dot_at(left, right):
    return lax.dot_general(left, right, (((0,), (0,)), ((), ())), preferred_element_type=F32)


def standardize(values):
    row_mean = jnp.mean(values, -1, keepdims=True)
    centred = values - row_mean
    inverse_deviation = lax.rsqrt(jnp.mean(centred * centred, -1, keepdims=True) + EPS)
    return centred * inverse_deviation, inverse_deviation


def norm_pull(grad_normed, gain, xhat, inverse_deviation):
    scaled = grad_normed * gain
    return inverse_deviation * (
        scaled
        - jnp.mean(scaled, -1, keepdims=True)
        - xhat * jnp.mean(scaled * xhat, -1, keepdims=True)
    )


def segment_bias(lengths_ref, seq, seq_len):
    end_one = lengths_ref[seq, 0]
    end_two = end_one + lengths_ref[seq, 1]
    end_three = end_two + lengths_ref[seq, 2]

    def ids(shape, dim):
        place = lax.broadcasted_iota(jnp.int32, shape, dim)
        return (
            (place >= end_one).astype(jnp.int32)
            + (place >= end_two).astype(jnp.int32)
            + (place >= end_three).astype(jnp.int32)
        )

    same = ids((seq_len, seq_len), 0) == ids((seq_len, seq_len), 1)
    return jnp.where(same, 0.0, MASKED).astype(F32)


def head_only(block, half):
    lane = lax.broadcasted_iota(jnp.int32, block.shape, 1)
    mine = (lane < HEAD_DIM) if half == 0 else (lane >= HEAD_DIM)
    return jnp.where(mine, block, jnp.zeros_like(block))


def attention_forward_kernel(
    seq_ref, lengths_ref, rows_ref, w_ref, b_ref, gain_ref, shift_ref,
    normed_ref, qkv_ref, attended_ref, lse_ref, bias_ref,
):
    seq_len = rows_ref.shape[0]
    width = w_ref.shape[2]
    xhat, _ = standardize(rows_ref[...])
    normed = (xhat * gain_ref[...] + shift_ref[...]).astype(BF16)
    normed_ref[...] = normed
    scale = 1.0 / math.sqrt(HEAD_DIM)
    qkv_ref[0] = ((dot(normed, w_ref[0]) + b_ref[0:1]).astype(BF16).astype(F32) * scale).astype(BF16)
    qkv_ref[1] = dot(normed, w_ref[1]).astype(BF16)
    qkv_ref[2] = (dot(normed, w_ref[2]) + b_ref[1:2]).astype(BF16)
    bias_ref[...] = segment_bias(lengths_ref, seq_ref[0], seq_len)
    lane = lax.broadcasted_iota(jnp.int32, (seq_len, LANES), 1)
    stats = jnp.zeros((seq_len, LANES), F32)
    for pair in range(width // LANES):
        cols = slice(pair * LANES, (pair + 1) * LANES)
        query, key, value = qkv_ref[0, :, cols], qkv_ref[1, :, cols], qkv_ref[2, :, cols]
        mixed = None
        for half in range(2):
            scores = dot_bt(query, head_only(key, half)) + bias_ref[...]
            row_max = jnp.max(scores, -1, keepdims=True)
            exps = jnp.exp(scores - row_max)
            total = jnp.sum(exps, -1, keepdims=True)
            probs = (exps * (1.0 / total)).astype(BF16)
            part = dot(probs, head_only(value, half))
            mixed = part if mixed is None else mixed + part
            stats = jnp.where(lane == 2 * pair + half, row_max + jnp.log(total), stats)
        attended_ref[:, cols] = mixed.astype(BF16).astype(F32)
    lse_ref[...] = stats.T[: lse_ref.shape[0]]


def attention_forward(seq, lengths, rows, w_heads, b_qv, gain, shift, seq_len):
    width = rows.shape[1]
    heads_width = w_heads.shape[2]
    stat_rows = 8 * pl.cdiv(heads_width // HEAD_DIM, 8)
    whole = lambda *shape: pl.BlockSpec(shape, lambda i, s, n: (0,) * len(shape))
    return pl.pallas_call(
        attention_forward_kernel,
        out_shape=(
            jax.ShapeDtypeStruct((seq_len, width), BF16),
            jax.ShapeDtypeStruct((3, seq_len, heads_width), BF16),
            jax.ShapeDtypeStruct((seq_len, heads_width), F32),
            jax.ShapeDtypeStruct((stat_rows, seq_len), F32),
        ),
        grid_spec=pltpu.PrefetchScalarGridSpec(
            num_scalar_prefetch=2,
            grid=(1,),
            in_specs=[
                pl.BlockSpec((seq_len, width), lambda i, s, n: (s[0], 0)),
                whole(3, width, heads_width),
                whole(2, heads_width),
                whole(1, width),
                whole(1, width),
            ],
            out_specs=[
                whole(seq_len, width),
                whole(3, seq_len, heads_width),
                whole(seq_len, heads_width),
                whole(stat_rows, seq_len),
            ],
            scratch_shapes=[pltpu.VMEM((seq_len, seq_len), F32)],
        ),
        compiler_params=pltpu.CompilerParams(vmem_limit_bytes=VMEM_BYTES),
        cost_estimate=pl.CostEstimate(
            flops=2 * seq_len * heads_width * (3 * width + 8 * seq_len),
            bytes_accessed=4 * seq_len * width + 6 * width * heads_width,
            transcendentals=seq_len * seq_len * heads_width // HEAD_DIM,
        ),
        name="attention_forward",
    )(seq, lengths, rows, w_heads, b_qv, gain, shift)


def feed_forward_kernel(
    seq_ref, rows_ref, cot_ref, att_mine_ref, att_peer_ref, wo_mine_ref, wo_peer_ref, b_out_ref,
    gain_ref, shift_ref, w_up_ref, b_up_ref, w_down_ref,
    middle_ref, normed_ref, hidden_ref, grad_pre_ref, down_ref, grad_normed_ref, grad_b_up_ref,
):
    middle = (
        rows_ref[...]
        + dot(att_mine_ref[...].astype(BF16), wo_mine_ref[...])
        + dot(att_peer_ref[...].astype(BF16), wo_peer_ref[...].astype(BF16))
        + b_out_ref[...]
    )
    middle_ref[...] = middle
    xhat, _ = standardize(middle)
    normed = (xhat * gain_ref[...] + shift_ref[...]).astype(BF16)
    normed_ref[...] = normed
    cot = cot_ref[...].astype(BF16)

    @pl.when(pl.program_id(0) == 0)
    def _():
        grad_b_up_ref[...] = jnp.zeros_like(grad_b_up_ref)

    pre = dot(normed, w_up_ref[...]) + b_up_ref[...]
    size = jnp.abs(pre) * math.sqrt(0.5)
    t = 1.0 / (1.0 + ERFC_P * size)
    gauss = jnp.exp(-0.5 * (pre * pre))
    poly = ERFC_C[-1]
    for c in ERFC_C[-2::-1]:
        poly = poly * t + c
    tail = 0.5 * (poly * t) * gauss
    cdf = jnp.where(pre >= 0, 1.0 - tail, tail)
    hidden = (pre * cdf).astype(BF16)
    slope = cdf + pre * gauss * (1.0 / math.sqrt(2.0 * math.pi))
    hidden_ref[...] = hidden
    down_ref[...] = dot(hidden, w_down_ref[...])
    grad_pre = (dot_bt(cot, w_down_ref[...]) * slope).astype(BF16)
    grad_pre_ref[...] = grad_pre
    grad_b_up_ref[...] += jnp.sum(grad_pre.astype(F32), 0, keepdims=True)
    grad_normed_ref[...] = dot_bt(grad_pre, w_up_ref[...])


def feed_forward(seq, rows, cot, att_mine, att_peer, wo_mine, wo_peer, b_out, gain, shift, w_up, b_up, w_down, seq_len):
    width = rows.shape[1]
    units = w_up.shape[1]
    heads_width = att_mine.shape[1]
    step = min(seq_len, 256)
    steps = seq_len // step
    whole = lambda *shape: pl.BlockSpec(shape, lambda i, s: (0,) * len(shape))
    local = lambda n: pl.BlockSpec((step, n), lambda i, s: (i, 0))
    chosen = lambda n: pl.BlockSpec((step, n), lambda i, s: (s[0] * steps + i, 0))
    return pl.pallas_call(
        feed_forward_kernel,
        out_shape=(
            jax.ShapeDtypeStruct((seq_len, width), F32),
            jax.ShapeDtypeStruct((seq_len, width), BF16),
            jax.ShapeDtypeStruct((seq_len, units), BF16),
            jax.ShapeDtypeStruct((seq_len, units), BF16),
            jax.ShapeDtypeStruct((seq_len, width), F32),
            jax.ShapeDtypeStruct((seq_len, width), F32),
            jax.ShapeDtypeStruct((1, units), F32),
        ),
        grid_spec=pltpu.PrefetchScalarGridSpec(
            num_scalar_prefetch=1,
            grid=(steps,),
            in_specs=[
                chosen(width),
                chosen(width),
                local(heads_width),
                local(heads_width),
                whole(heads_width, width),
                whole(heads_width, width),
                whole(1, width),
                whole(1, width),
                whole(1, width),
                whole(width, units),
                whole(1, units),
                whole(units, width),
            ],
            out_specs=[
                local(width), local(width), local(units), local(units), local(width), local(width), whole(1, units),
            ],
        ),
        compiler_params=pltpu.CompilerParams(vmem_limit_bytes=VMEM_BYTES),
        cost_estimate=pl.CostEstimate(
            flops=2 * seq_len * width * (4 * units + 2 * heads_width),
            bytes_accessed=4 * units * width + 22 * seq_len * width,
            transcendentals=seq_len * units,
        ),
        name="feed_forward",
    )(seq, rows, cot, att_mine, att_peer, wo_mine, wo_peer, b_out, gain, shift, w_up, b_up, w_down)


def middle_gradient_kernel(
    seq_ref, mine_ref, peer_ref, middle_ref, cot_ref, gain_ref, grad_middle_ref, sums_ref,
):
    grad_normed = mine_ref[...] + peer_ref[...]
    cot = cot_ref[...]
    xhat, inverse_deviation = standardize(middle_ref[...])
    grad_middle = cot + norm_pull(grad_normed, gain_ref[...], xhat, inverse_deviation)
    grad_middle_ref[...] = grad_middle

    def total(values):
        return jnp.sum(values, 0, keepdims=True)

    sums_ref[...] = jnp.concatenate(
        [total(grad_normed * xhat), total(grad_normed), total(grad_middle), total(cot)]
        + [jnp.zeros_like(gain_ref[...])] * 4,
        axis=0,
    )


def input_gradient_kernel(
    seq_ref, mine_ref, peer_ref, rows_ref, grad_middle_ref, gain_ref, grad_rows_ref, sums_ref,
):
    grad_normed = mine_ref[...] + peer_ref[...]
    xhat, inverse_deviation = standardize(rows_ref[...])
    grad_rows_ref[...] = grad_middle_ref[...] + norm_pull(grad_normed, gain_ref[...], xhat, inverse_deviation)

    def total(values):
        return jnp.sum(values, 0, keepdims=True)

    sums_ref[...] = jnp.concatenate(
        [total(grad_normed * xhat), total(grad_normed)] + [jnp.zeros_like(gain_ref[...])] * 6, axis=0
    )


def norm_gradient(kernel, seq, mine, peer, third, fourth, gain, chosen, seq_len, name):
    width = mine.shape[1]
    own = pl.BlockSpec((seq_len, width), lambda i, s: (0, 0))
    pick = pl.BlockSpec((seq_len, width), lambda i, s: (s[0], 0))
    return pl.pallas_call(
        kernel,
        out_shape=(jax.ShapeDtypeStruct((seq_len, width), F32), jax.ShapeDtypeStruct((8, width), F32)),
        grid_spec=pltpu.PrefetchScalarGridSpec(
            num_scalar_prefetch=1,
            grid=(1,),
            in_specs=[own, own, pick if chosen == 2 else own, pick if chosen == 3 else own,
                      pl.BlockSpec((1, width), lambda i, s: (0, 0))],
            out_specs=[own, pl.BlockSpec((8, width), lambda i, s: (0, 0))],
        ),
        compiler_params=pltpu.CompilerParams(vmem_limit_bytes=VMEM_BYTES),
        cost_estimate=pl.CostEstimate(flops=20 * seq_len * width, bytes_accessed=20 * seq_len * width, transcendentals=seq_len),
        name=name,
    )(seq, mine, peer, third, fourth, gain)


def attention_backward_kernel(
    seq_ref, lengths_ref, grad_middle_ref, qkv_ref, lse_ref, w_out_ref, w_ref,
    grad_qkv_ref, grad_normed_ref, sums_ref, bias_ref, grad_att_ref,
):
    seq_len = grad_middle_ref.shape[0]
    width = w_ref.shape[2]
    grad_att_ref[...] = dot_bt(grad_middle_ref[...].astype(BF16), w_out_ref[...]).astype(BF16)
    bias_ref[...] = segment_bias(lengths_ref, seq_ref[0], seq_len)
    scale = 1.0 / math.sqrt(HEAD_DIM)
    for pair in range(width // LANES):
        cols = slice(pair * LANES, (pair + 1) * LANES)
        query, key, value = qkv_ref[0, :, cols], qkv_ref[1, :, cols], qkv_ref[2, :, cols]
        grad_att = grad_att_ref[:, cols]
        grad_query = grad_key = grad_value = 0.0
        for half in range(2):
            head = 2 * pair + half
            key_half = head_only(key, half)
            scores = dot_bt(key_half, query) + bias_ref[...]
            probs = jnp.exp(scores - lse_ref[head : head + 1, :])
            grad_probs = dot_bt(head_only(value, half), grad_att)
            inner = jnp.sum(grad_probs * probs, 0, keepdims=True)
            grad_scores = (probs * (grad_probs - inner)).astype(BF16)
            grad_value += dot(probs.astype(BF16), head_only(grad_att, half))
            grad_key += dot(grad_scores, head_only(query, half))
            grad_query += dot_at(grad_scores, key_half)
        grad_qkv_ref[0, :, cols] = (grad_query * scale).astype(BF16)
        grad_qkv_ref[1, :, cols] = grad_key.astype(BF16)
        grad_qkv_ref[2, :, cols] = grad_value.astype(BF16)
    grad_normed_ref[...] = (
        dot_bt(grad_qkv_ref[0], w_ref[0]) + dot_bt(grad_qkv_ref[1], w_ref[1]) + dot_bt(grad_qkv_ref[2], w_ref[2])
    )
    sums_ref[...] = jnp.concatenate(
        [jnp.sum(grad_qkv_ref[0].astype(F32), 0, keepdims=True), jnp.sum(grad_qkv_ref[2].astype(F32), 0, keepdims=True)]
        + [jnp.zeros((6, width), F32)],
        axis=0,
    )


def attention_backward(seq, lengths, grad_middle, qkv, lse, w_out, w_heads):
    seq_len, width = grad_middle.shape
    heads_width = w_heads.shape[2]
    whole = lambda *shape: pl.BlockSpec(shape, lambda i, s, n: (0,) * len(shape))
    return pl.pallas_call(
        attention_backward_kernel,
        out_shape=(
            jax.ShapeDtypeStruct((3, seq_len, heads_width), BF16),
            jax.ShapeDtypeStruct((seq_len, width), F32),
            jax.ShapeDtypeStruct((8, heads_width), F32),
        ),
        grid_spec=pltpu.PrefetchScalarGridSpec(
            num_scalar_prefetch=2,
            grid=(1,),
            in_specs=[
                whole(seq_len, width),
                whole(3, seq_len, heads_width),
                whole(*lse.shape),
                whole(heads_width, width),
                whole(3, width, heads_width),
            ],
            out_specs=[whole(3, seq_len, heads_width), whole(seq_len, width), whole(8, heads_width)],
            scratch_shapes=[pltpu.VMEM((seq_len, seq_len), F32), pltpu.VMEM((seq_len, heads_width), BF16)],
        ),
        compiler_params=pltpu.CompilerParams(vmem_limit_bytes=VMEM_BYTES),
        cost_estimate=pl.CostEstimate(
            flops=2 * seq_len * heads_width * (4 * width + 20 * seq_len),
            bytes_accessed=8 * seq_len * width + 8 * width * heads_width,
            transcendentals=seq_len * seq_len * heads_width // HEAD_DIM,
        ),
        name="attention_backward",
    )(seq, lengths, grad_middle, qkv, lse, w_out, w_heads)


def swap(values):
    return lax.ppermute(values, "tensor", [(0, 1), (1, 0)])


def exchange(values, stride, count):
    return lax.ppermute(values, "dp", [(i, i ^ stride) for i in range(count)])


def sum_over_dp(part, place, count):
    strides = [1 << i for i in range(count.bit_length() - 1)]
    taken = []
    for stride in strides:
        half = part.shape[0] // 2
        if stride != strides[-1] and part.shape[0] % 32 == 0:
            bit = (place // stride) % 2
            sent = lax.dynamic_slice_in_dim(part, (1 - bit) * half, half, 0)
            kept = lax.dynamic_slice_in_dim(part, bit * half, half, 0)
            part = kept + exchange(sent, stride, count)
            taken.append((stride, bit))
        else:
            part = part + exchange(part, stride, count)
    for stride, bit in reversed(taken):
        got = exchange(part, stride, count)
        size = part.shape[0]
        both = jnp.zeros((2 * size,) + part.shape[1:], part.dtype)
        both = lax.dynamic_update_slice_in_dim(both, part, bit * size, 0)
        part = lax.dynamic_update_slice_in_dim(both, got, (1 - bit) * size, 0)
    return part


def shards(dp_count, inputs, pair_lengths, first_norm_gain, first_norm_bias, w_qkv, b_qv, w_out, b_out,
           second_norm_gain, second_norm_bias, w_up, b_up, w_down, b_down, cotangent):
    seq_count = pair_lengths.shape[0]
    token_count, width = inputs.shape
    seq_len = token_count // seq_count
    heads_width = w_qkv.shape[2]
    units = w_up.shape[1]
    side = lax.axis_index("tensor")
    place = lax.axis_index("dp")
    own, other = side.astype(jnp.int32).reshape(1), (1 - side).astype(jnp.int32).reshape(1)
    w_heads = w_qkv.transpose(1, 0, 2)
    gain_one, shift_one = first_norm_gain.reshape(1, width), first_norm_bias.reshape(1, width)
    gain_two, shift_two = second_norm_gain.reshape(1, width), second_norm_bias.reshape(1, width)
    b_out_row, b_up_row = b_out.reshape(1, width), b_up.reshape(1, units)

    core = place % 2
    piece_rows = heads_width // 2
    piece = lax.dynamic_slice_in_dim(w_out, core * piece_rows, piece_rows, 0).astype(F32)
    piece = swap(piece)
    piece_two = exchange(piece, 1, dp_count)
    wo_peer = jnp.where(core == 0, jnp.concatenate([piece, piece_two]), jnp.concatenate([piece_two, piece]))

    def forward(seq):
        return attention_forward(seq, pair_lengths, inputs, w_heads, b_qv, gain_one, shift_one, seq_len)

    normed_own, qkv_own, att_own, lse_own = forward(own)
    att_peer_other = swap(att_own)
    normed_other, qkv_other, att_other, lse_other = forward(other)
    att_peer_own = swap(att_other)

    def feed(seq, att_mine, att_peer):
        return feed_forward(seq, inputs, cotangent, att_mine, att_peer, w_out, wo_peer, b_out_row, gain_two, shift_two,
                            w_up, b_up_row, w_down, seq_len)

    _, normed_two_other, hidden_other, grad_pre_other, down_other, gn_two_other, b_up_other = feed(other, att_other, att_peer_other)
    gn_two_peer = swap(gn_two_other)
    middle, normed_two_own, hidden_own, grad_pre_own, down_own, gn_two_own, b_up_own = feed(own, att_own, att_peer_own)

    rows_of = lambda values, seq: lax.dynamic_slice_in_dim(values, seq[0] * seq_len, seq_len, 0)
    cot_own, cot_other = rows_of(cotangent, own).astype(BF16), rows_of(cotangent, other).astype(BF16)
    grad_w_down = dot_at(hidden_own, cot_own) + dot_at(hidden_other, cot_other)
    grad_w_up = dot_at(normed_two_own, grad_pre_own) + dot_at(normed_two_other, grad_pre_other)
    grad_w_down = sum_over_dp(grad_w_down, place, dp_count)
    grad_w_up = sum_over_dp(grad_w_up, place, dp_count)

    grad_middle_own, sums_two = norm_gradient(
        middle_gradient_kernel, own, gn_two_own, gn_two_peer, middle, cotangent, gain_two, 3, seq_len, "middle_gradient")
    grad_middle_other = swap(grad_middle_own)

    def backward(seq, grad_middle, qkv, lse):
        return attention_backward(seq, pair_lengths, grad_middle, qkv, lse, w_out, w_heads)

    grad_qkv_own, gn_one_own, b_qv_own = backward(own, grad_middle_own, qkv_own, lse_own)
    grad_qkv_other, gn_one_other, b_qv_other = backward(other, grad_middle_other, qkv_other, lse_other)
    gn_one_peer = swap(gn_one_other)
    grad_w_out = dot_at(att_own.astype(BF16), grad_middle_own.astype(BF16)) + dot_at(
        att_other.astype(BF16), grad_middle_other.astype(BF16))
    grad_w_heads = jnp.concatenate(
        [dot_at(normed_own, grad_qkv_own[j]) + dot_at(normed_other, grad_qkv_other[j]) for j in range(3)])
    grad_w_out = sum_over_dp(grad_w_out, place, dp_count)
    grad_w_heads = sum_over_dp(grad_w_heads, place, dp_count)

    grad_inputs_own, sums_one = norm_gradient(
        input_gradient_kernel, own, gn_one_own, gn_one_peer, inputs, grad_middle_own, gain_one, 2, seq_len, "input_gradient")
    grad_inputs_other = swap(grad_inputs_own)

    down_peer = swap(down_other)
    output_own = middle + (down_own + down_peer) + b_down
    output_other = swap(output_own)

    def whole_rows(mine, peer):
        both = jnp.zeros((token_count, width), F32)
        both = lax.dynamic_update_slice_in_dim(both, mine, own[0] * seq_len, 0)
        return lax.dynamic_update_slice_in_dim(both, peer, other[0] * seq_len, 0)

    sums = jnp.concatenate([sums_two[:4], sums_one[:2]])
    sums = sums + swap(sums)
    b_qv_sum = (b_qv_own + b_qv_other)[:2]
    wide = max(width, units, 2 * heads_width)
    row = lambda values: jnp.pad(values.reshape(1, -1), ((0, 0), (0, wide - values.size)))
    small = jnp.concatenate([row(sums[i]) for i in range(6)] + [row(b_up_own + b_up_other), row(b_qv_sum)])
    small = sum_over_dp(small, place, dp_count)
    return (
        whole_rows(output_own, output_other),
        whole_rows(grad_inputs_own, grad_inputs_other),
        small[4, :width],
        small[5, :width],
        grad_w_heads.reshape(3, width, heads_width).transpose(1, 0, 2),
        small[7, : 2 * heads_width].reshape(2, heads_width),
        grad_w_out,
        small[2, :width],
        small[0, :width],
        small[1, :width],
        grad_w_up,
        small[6, :units],
        grad_w_down,
        small[3, :width],
    )


def solution(mesh):
    rows, copied, columns = P("dp", None), P(), P(None, "tensor")
    heads, split_rows = P(None, None, "tensor"), P("tensor", None)
    return jax.shard_map(
        functools.partial(shards, mesh.shape["dp"]),
        mesh=mesh,
        in_specs=(rows, rows, copied, copied, heads, columns, split_rows, copied, copied, copied, columns,
                  P("tensor"), split_rows, copied, rows),
        out_specs=(rows, rows, copied, copied, heads, columns, split_rows, copied, copied, copied, columns,
                   P("tensor"), split_rows, copied),
        check_vma=False,
    )
```

time: 1110 us -> 408 us (0.37)
  waiting for transfers between devices: 801 us -> 101 us
  starting transfers between devices: 0.82 us -> 117 us
  matrix products: 106 us -> 20.3 us
  Pallas kernels: 0 us -> 79.3 us
  local copies, waits for them, and re-layouts: 143 us -> 63.8 us
  other arithmetic: 34.7 us -> 15.9 us
  between operations: 17.7 us -> 2.01 us
    unnamed x12 -> x0, waiting for transfers between devices: 511 us -> none
    all_gather x4 -> x0, waiting for transfers between devices: 169 us -> none  [the longest x1 46.5 us: shards(): lax.all_gather(lax.psum_scatter(branch, 'tensor', scatter_dimension=0, ti...]
    reduce_scatter x4 -> x0, waiting for transfers between devices: 121 us -> none  [the longest x1 45.5 us: shards(): lax.psum_scatter(branch, 'tensor', scatter_dimension=0, tiled=True)]
    ppermute x0 -> x43, starting transfers between devices: none -> 117 us  [the longest x33 101 us: exchange(): return lax.ppermute(values, 'dp', [(i, i ^ stride) for i in range(count)])]
    ppermute x0 -> x43, waiting for transfers between devices: none -> 101 us  [the longest x33 72.2 us: exchange(): return lax.ppermute(values, 'dp', [(i, i ^ stride) for i in range(count)])]
    dot_general x26 -> x12, matrix products: 106 us -> 20.3 us  [dot_at(): lax.dot_general(left, right, (((0,), (0,)), ((), ())), preferred_element_...]
    pallas_call x0 -> x8, Pallas kernels: none -> 79.3 us  [the longest x2 29.4 us: feed_forward(): pl.pallas_call(feed_forward_kernel, out_shape=(jax.ShapeDtypeStruct((seq_...]
    unnamed x88 -> x89, local copies, waits for them, and re-layouts: 48.2 us -> 9.12 us
  transfers between devices with their start and end apart: 10 -> 43, of which waited for: 10 -> 16; matrix products, arithmetic and copies ran while one was open for 7% -> 22% of each run, Pallas kernels for 0% -> 20%
where the time goes in v2:
time: 408 us; the launch traced here: 400 us
  starting transfers between devices  117 us (29%)
  waiting for transfers between devices  101 us (25%)
  Pallas kernels  79.3 us (19%)
  local copies, waits for them, and re-layouts  63.8 us (16%)
  matrix products  20.3 us (5%)
  other arithmetic  15.9 us (4%)
    ppermute x33, starting transfers between devices, exchange(): return lax.ppermute(values, 'dp', [(i, i ^ stride) for i in range(count)])  101 us
    ppermute x33, waiting for transfers between devices, exchange(): return lax.ppermute(values, 'dp', [(i, i ^ stride) for i in range(count)])  72.2 us
    pallas_call x2, Pallas kernels, feed_forward(): pl.pallas_call(feed_forward_kernel, out_shape=(jax.ShapeDtypeStruct((seq_...  29.4 us
    ppermute x10, waiting for transfers between devices, swap(): return lax.ppermute(values, 'tensor', [(0, 1), (1, 0)])  29 us
    pallas_call x2, Pallas kernels, attention_backward(): pl.pallas_call(attention_backward_kernel, out_shape=(jax.ShapeDtypeStruct...  22.6 us
    dot_general x12, matrix products, dot_at(): lax.dot_general(left, right, (((0,), (0,)), ((), ())), preferred_element_...  20.3 us
    pallas_call x2, Pallas kernels, attention_forward(): pl.pallas_call(attention_forward_kernel, out_shape=(jax.ShapeDtypeStruct(...  16.9 us
    ppermute x10, starting transfers between devices, swap(): return lax.ppermute(values, 'tensor', [(0, 1), (1, 0)])  16.5 us
  transfers between devices with their start and end apart: 43, of which 16 were waited for; matrix products, arithmetic and copies ran while one was open for 22% of the time, Pallas kernels for 20%

profile of v2, /device:TPU:1, one launch (start us, length us, event | category | flops | bytes accessed | tf_op | source)
XLA Modules:
  0.0 399.6 jit_solution(8735646159445502045)
XLA Ops:
  1.7 2.1 collective-permute-start.1
  6.3 8.4 %attention_forward.2 = (bf16[512,768]{1,0:T(8,128)(2,1)}, bf16[3,512,384]{2,1,0:T(8,128)(2,1)}, f32[512,384]{1,0:T(8,128)}, f32[8,512]{1,0:T(8,128)}) custom-call(s32[1]{0:T(128)} %bitcast.seq_ref, s32[2,3]{1,0:T(2,128)} %lengths_ref.7, f32[1024,768]{1,0:T(8,128)} %rows_ref.9, bf16[3,768,384]{2,1,0:T(8,128)(2,1)} %bitcast.46, f32[2,384]{1,0:T(2,128)} %b_ref.3, ...), custom_call_target="tpu_custom_call" | custom-call | flops 2516582400 | bytes 3342336 | tf_op jit(solution)/shard_map/attention_forward/pallas_call | solution.py:118
  14.7 2.1 collective-permute-done.1
  16.8 1.6 collective-permute-start.2
  18.5 8.5 %attention_forward.3 = (bf16[512,768]{1,0:T(8,128)(2,1)}, bf16[3,512,384]{2,1,0:T(8,128)(2,1)}, f32[512,384]{1,0:T(8,128)}, f32[8,512]{1,0:T(8,128)}) custom-call(s32[1]{0:T(128)} %bitcast.2.seq_ref, s32[2,3]{1,0:T(2,128)} %lengths_ref.7, f32[1024,768]{1,0:T(8,128)} %rows_ref.9, bf16[3,768,384]{2,1,0:T(8,128)(2,1)} %bitcast.47, f32[2,384]{1,0:T(2,128)} %b_ref.3, ...), custom_call_target="tpu_custom_call" | custom-call | flops 2516582400 | bytes 3342336 | tf_op jit(solution)/shard_map/attention_forward/pallas_call | solution.py:118
  27.0 2.2 collective-permute-start
  34.0 14.9 %feed_forward.3 = (f32[512,768]{1,0:T(8,128)}, bf16[512,768]{1,0:T(8,128)(2,1)}, bf16[512,1536]{1,0:T(8,128)(2,1)}, bf16[512,1536]{1,0:T(8,128)(2,1)}, f32[512,7...) custom-call(s32[1]{0:T(128)} %bitcast.2.seq_ref, f32[1024,768]{1,0:T(8,128)} %rows_ref.9, f32[1024,768]{1,0:T(8,128)} %cot_ref.5, ...), custom_call_target="tpu_custom_call" | custom-call | flops 5435817984 | bytes 13369344 | tf_op jit(solution)/shard_map/feed_forward/pallas_call | solution.py:203
  48.9 1.8 collective-permute-start.6
  50.8 3.3 fusion
  54.1 14.5 %feed_forward.2 = (f32[512,768]{1,0:T(8,128)}, bf16[512,768]{1,0:T(8,128)(2,1)}, bf16[512,1536]{1,0:T(8,128)(2,1)}, bf16[512,1536]{1,0:T(8,128)(2,1)}, f32[512,7...) custom-call(s32[1]{0:T(128)} %bitcast.seq_ref, f32[1024,768]{1,0:T(8,128)} %rows_ref.9, f32[1024,768]{1,0:T(8,128)} %cot_ref.5, ...), custom_call_target="tpu_custom_call" | custom-call | flops 5435817984 | bytes 13369344 | tf_op jit(solution)/shard_map/feed_forward/pallas_call | solution.py:203
  68.6 3.4 convolution_add_fusion
  72.0 1.6 constant_dynamic-slice_fusion.2
  73.6 1.5 copy-done
  75.1 3.4 collective-permute-start.36
  81.7 1.7 constant_dynamic-slice_fusion.5
  86.5 5.3 %middle_gradient.1 = (f32[512,768]{1,0:T(8,128)}, f32[8,768]{1,0:T(8,128)}) custom-call(s32[1]{0:T(128)} %bitcast.seq_ref, f32[512,768]{1,0:T(8,128)} %get-tuple-element.50.mine_ref, f32[512,768]{1,0:T(8,128)} %copy-done.19, f32[512,768]{1,0:T(8,128)} %get-tuple-element.47.middle_ref, f32[1024,768]{1,0:T(8,128)} %cot_ref.5, f32[1,768]{1,0:T(1,128)} %reshape.64.gain_ref), custom_call_target="tpu_custom_call" | custom-call | flops 7864320 | bytes 7864320 | tf_op jit(solution)/shard_map/middle_gradient/pallas_call | solution.py:283
  93.7 22.3 %collective-permute-done.4 = f32[512,768]{1,0:T(8,128)S(1)} collective-permute-done((f32[512,768]{1,0:T(8,128)}, f32[512,768]{1,0:T(8,128)S(1)}, u32[]{:S(2)}, u32[]{:S(2)}) %collective-permute-start.4) | collective-permute-done | bytes 1572896 | tf_op jit(solution)/shard_map/ppermute | solution.py:372
  119.5 1.7 collective-permute-start.5
  121.2 11.4 %attention_backward.2 = (bf16[3,512,384]{2,1,0:T(8,128)(2,1)}, f32[512,768]{1,0:T(8,128)}, f32[8,384]{1,0:T(8,128)}) custom-call(s32[1]{0:T(128)} %bitcast.seq_ref, s32[2,3]{1,0:T(2,128)} %lengths_ref.7, f32[512,768]{1,0:T(8,128)} %get-tuple-element.52.grad_middle_ref, bf16[3,512,384]{2,1,0:T(8,128)(2,1)} %get-tuple-element.53.qkv_ref, ...), custom_call_target="tpu_custom_call" | custom-call | flops 5234491392 | bytes 5505024 | tf_op jit(solution)/shard_map/attention_backward/pallas_call | solution.py:341
  132.6 2.7 fusion.11
  135.3 1.7 fusion.8
  137.7 2.3 dynamic-slice_add_fusion
  141.0 1.7 collective-permute-start.37
  142.7 2.0 dynamic-slice_add_fusion.1
  145.9 4.0 %collective-permute-done.7.grad_middle_ref = f32[512,768]{1,0:T(8,128)} collective-permute-done((f32[512,768]{1,0:T(8,128)}, f32[512,768]{1,0:T(8,128)}, u32[]{:S(2)}, u32[]{:S(2)}) %collective-permute-start.7) | collective-permute-done | bytes 1572896 | tf_op jit(solution)/shard_map/ppermute | solution.py:372
  149.9 1.9 fusion.1
  153.3 7.3 %collective-permute-start.22 = (f32[192,768]{1,0:T(8,128)}, f32[192,768]{1,0:T(8,128)}, u32[]{:S(2)}, u32[]{:S(2)}) collective-permute-start(f32[192,768]{1,0:T(8,128)} %constant_dynamic-slice_fusion.8), channel_id=1, source_target_pairs={{0,2},{2,0},{4,6},{6,4},{8,10},{10,8},{12,14},{14,12},{16,18},{18,... | collective-permute-start | bytes 1769480 | tf_op jit(solution)/shard_map/ppermute | solution.py:376
  160.7 11.2 %attention_backward.3 = (bf16[3,512,384]{2,1,0:T(8,128)(2,1)}, f32[512,768]{1,0:T(8,128)}, f32[8,384]{1,0:T(8,128)}) custom-call(s32[1]{0:T(128)} %bitcast.2.seq_ref, s32[2,3]{1,0:T(2,128)} %lengths_ref.7, f32[512,768]{1,0:T(8,128)} %collective-permute-done.7.grad_middle_ref, bf16[3,512,384]{2,1,0:T(8,128)(2,1)} %get-tuple-element.56.qkv_ref, ...), custom_call_target="tpu_custom_call" | custom-call | flops 5234491392 | bytes 5505024 | tf_op jit(solution)/shard_map/attention_backward/pallas_call | solution.py:341
  171.9 2.1 convolution_add_fusion.5
  182.8 4.4 %collective-permute-done.30 = f32[192,1536]{1,0:T(8,128)} collective-permute-done((f32[192,1536]{1,0:T(8,128)}, f32[192,1536]{1,0:T(8,128)}, u32[]{:S(2)}, u32[]{:S(2)}) %collective-permute-start.30) | collective-permute-done | bytes 1179680 | tf_op jit(solution)/shard_map/ppermute | solution.py:376
  187.2 1.7 collective-permute-start.23
  190.4 6.3 %collective-permute-done.23 = f32[96,768]{1,0:T(8,128)S(1)} collective-permute-done((f32[96,768]{1,0:T(8,128)S(1)}, f32[96,768]{1,0:T(8,128)S(1)}, u32[]{:S(2)}, u32[]{:S(2)}) %collective-permute-start.23) | collective-permute-done | bytes 294944 | tf_op jit(solution)/shard_map/ppermute | solution.py:376
  196.6 1.5 collective-permute-start.31
  198.4 9.0 %collective-permute-done.24 = f32[48,768]{1,0:T(8,128)S(1)} collective-permute-done((f32[48,768]{1,0:T(8,128)S(1)}, f32[48,768]{1,0:T(8,128)S(1)}, u32[]{:S(2)}, u32[]{:S(2)}) %collective-permute-start.24) | collective-permute-done | bytes 147488 | tf_op jit(solution)/shard_map/ppermute | solution.py:376
  207.4 2.5 collective-permute-start.39
  211.8 23.5 %collective-permute-done.25 = f32[48,768]{1,0:T(8,128)S(1)} collective-permute-done((f32[48,768]{1,0:T(8,128)S(1)}, f32[48,768]{1,0:T(8,128)S(1)}, u32[]{:S(2)}, u32[]{:S(2)}) %collective-permute-start.25) | collective-permute-done | bytes 147488 | tf_op jit(solution)/shard_map/ppermute | solution.py:376
  235.9 4.3 %collective-permute-start.26 = (f32[48,768]{1,0:T(8,128)}, f32[48,768]{1,0:T(8,128)S(1)}, u32[]{:S(2)}, u32[]{:S(2)}) collective-permute-start(f32[48,768]{1,0:T(8,128)} %get-tuple-element.88), channel_id=1, source_target_pairs={{0,8},{2,10},{4,12},{6,14},{8,0},{10,2},{12,4},{14,6},{16,24},{18,... | collective-permute-start | bytes 442376 | tf_op jit(solution)/shard_map/ppermute | solution.py:376
  240.5 5.1 %input_gradient.1 = (f32[512,768]{1,0:T(8,128)}, f32[8,768]{1,0:T(8,128)}) custom-call(s32[1]{0:T(128)} %bitcast.seq_ref, f32[512,768]{1,0:T(8,128)} %get-tuple-element.55.mine_ref, f32[512,768]{1,0:T(8,128)} %collective-permute-done.8.peer_ref, f32[1024,768]{1,0:T(8,128)} %rows_ref.9, f32[512,768]{1,0:T(8,128)} %get-tuple-element.52.grad_middle_ref, ...), custom_call_target="tpu_custom_call" | custom-call | flops 7864320 | bytes 7864320 | tf_op jit(solution)/shard_map/input_gradient/pallas_call | solution.py:283
  247.8 7.5 %collective-permute-done.32 = f32[96,1536]{1,0:T(8,128)S(1)} collective-permute-done((f32[96,1536]{1,0:T(8,128)S(1)}, f32[96,1536]{1,0:T(8,128)S(1)}, u32[]{:S(2)}, u32[]{:S(2)}) %collective-permute-start.32) | collective-permute-done | bytes 589856 | tf_op jit(solution)/shard_map/ppermute | solution.py:376
  255.3 7.1 %collective-permute-start.17 = (f32[288,384]{1,0:T(8,128)S(1)}, f32[288,384]{1,0:T(8,128)S(1)}, u32[]{:S(2)}, u32[]{:S(2)}) collective-permute-start(f32[288,384]{1,0:T(8,128)S(1)} %constant_dynamic-slice_fusion.9), channel_id=1, source_target_pairs={{0,8},{2,10},{4,12},{6,14},{8,0},{10,2},{12,4},{14,6},{16,24},{18,... | collective-permute-start | bytes 1327112 | tf_op jit(solution)/shard_map/ppermute | solution.py:376
  265.7 4.4 %collective-permute-done.17 = f32[288,384]{1,0:T(8,128)S(1)} collective-permute-done((f32[288,384]{1,0:T(8,128)S(1)}, f32[288,384]{1,0:T(8,128)S(1)}, u32[]{:S(2)}, u32[]{:S(2)}) %collective-permute-start.17) | collective-permute-done | bytes 442400 | tf_op jit(solution)/shard_map/ppermute | solution.py:376
  270.1 9.9 %collective-permute-start.18 = (f32[288,384]{1,0:T(8,128)S(1)}, f32[288,384]{1,0:T(8,128)S(1)}, u32[]{:S(2)}, u32[]{:S(2)}) collective-permute-start(f32[288,384]{1,0:T(8,128)S(1)} %dynamic-slice_add_fusion.9), channel_id=1, source_target_pairs={{0,16},{2,18},{4,20},{6,22},{8,24},{10,26},{12,28},{14,30},{16,0},... | collective-permute-start | bytes 1327112 | tf_op jit(solution)/shard_map/ppermute | solution.py:376
  280.0 7.6 %collective-permute-done.33 = f32[96,1536]{1,0:T(8,128)S(1)} collective-permute-done((f32[96,1536]{1,0:T(8,128)S(1)}, f32[96,1536]{1,0:T(8,128)S(1)}, u32[]{:S(2)}, u32[]{:S(2)}) %collective-permute-start.33) | collective-permute-done | bytes 589856 | tf_op jit(solution)/shard_map/ppermute | solution.py:376
  288.4 4.1 %collective-permute-start.34 = (f32[192,1536]{1,0:T(8,128)}, f32[192,1536]{1,0:T(8,128)}, u32[]{:S(2)}, u32[]{:S(2)}) collective-permute-start(f32[192,1536]{1,0:T(8,128)} %constant_dynamic-update-slice_fusion.10), channel_id=1, source_target_pairs={{0,4},{2,6},{4,0},{6,2},{8,12},{10,14},{12,8},{14,10},{16,20},{18,... | collective-permute-start | bytes 3538952 | tf_op jit(solution)/shard_map/ppermute | solution.py:376
  292.7 10.6 %collective-permute-start.11 = (f32[8,1536]{1,0:T(8,128)S(1)}, f32[8,1536]{1,0:T(8,128)S(1)}, u32[]{:S(2)}, u32[]{:S(2)}) collective-permute-start(f32[8,1536]{1,0:T(8,128)S(1)} %concatenate.18), channel_id=1, source_target_pairs={{0,2},{2,0},{4,6},{6,4},{8,10},{10,8},{12,14},{14,12},{16,18},{18,... | collective-permute-start | bytes 147464 | tf_op jit(solution)/shard_map/ppermute | solution.py:376
  304.2 5.0 %collective-permute-start.9 = (f32[512,768]{1,0:T(8,128)}, f32[512,768]{1,0:T(8,128)}, u32[]{:S(2)}, u32[]{:S(2)}) collective-permute-start(f32[512,768]{1,0:T(8,128)} %get-tuple-element.59), channel_id=1, source_target_pairs={{0,1},{1,0},{2,3},{3,2},{4,5},{5,4},{6,7},{7,6},{8,9},{9,8},{10,11... | collective-permute-start | bytes 4718600 | tf_op jit(solution)/shard_map/ppermute | solution.py:372
  309.7 1.7 broadcast_in_dim.37
  311.3 2.4 constant_dynamic-update-slice_fusion.9
  315.1 3.0 collective-permute-done.19
  318.1 4.4 %collective-permute-start.42 = (f32[768,768]{1,0:T(8,128)S(1)}, f32[768,768]{1,0:T(8,128)}, u32[]{:S(2)}, u32[]{:S(2)}) collective-permute-start(f32[768,768]{1,0:T(8,128)S(1)} %constant_dynamic-update-slice_fusion.2), channel_id=1, source_target_pairs={{0,2},{2,0},{4,6},{6,4},{8,10},{10,8},{12,14},{14,12},{16,18},{18,... | collective-permute-start | bytes 7077896 | tf_op jit(solution)/shard_map/ppermute | solution.py:376
  322.6 2.5 constant_dynamic-update-slice_fusion.8
  326.5 16.1 %collective-permute-start.35 = (f32[384,1536]{1,0:T(8,128)}, f32[384,1536]{1,0:T(8,128)}, u32[]{:S(2)}, u32[]{:S(2)}) collective-permute-start(f32[384,1536]{1,0:T(8,128)} %constant_dynamic-update-slice_fusion.8), channel_id=1, source_target_pairs={{0,2},{2,0},{4,6},{6,4},{8,10},{10,8},{12,14},{14,12},{16,18},{18,... | collective-permute-start | bytes 7077896 | tf_op jit(solution)/shard_map/ppermute | solution.py:376
  344.4 2.3 constant_dynamic-update-slice_fusion.25
  348.0 3.2 collective-permute-done.13
  351.2 10.6 %collective-permute-start.28 = (f32[192,768]{1,0:T(8,128)S(1)}, f32[192,768]{1,0:T(8,128)S(1)}, u32[]{:S(2)}, u32[]{:S(2)}) collective-permute-start(f32[192,768]{1,0:T(8,128)S(1)} %constant_dynamic-update-slice_fusion.14), channel_id=1, source_target_pairs={{0,2},{2,0},{4,6},{6,4},{8,10},{10,8},{12,14},{14,12},{16,18},{18,... | collective-permute-start | bytes 1769480 | tf_op jit(solution)/shard_map/ppermute | solution.py:376
  364.1 7.4 %collective-permute-start.14 = (f32[8,1536]{1,0:T(8,128)S(1)}, f32[8,1536]{1,0:T(8,128)S(1)}, u32[]{:S(2)}, u32[]{:S(2)}) collective-permute-start(f32[8,1536]{1,0:T(8,128)S(1)} %add.258), channel_id=1, source_target_pairs={{0,16},{2,18},{4,20},{6,22},{8,24},{10,26},{12,28},{14,30},{16,0},... | collective-permute-start | bytes 147464 | tf_op jit(solution)/shard_map/ppermute | solution.py:376
  373.6 1.6 collective-permute-start.21
  381.3 2.7 constant_dynamic-update-slice_fusion.24
  385.1 1.9 constant_dynamic-update-slice_fusion.7
  387.2 1.6 constant_dynamic-update-slice_fusion.19
  388.8 1.9 constant_dynamic-update-slice_fusion
  390.7 3.6 constant_dynamic-update-slice_fusion.6
  394.4 2.9 constant_dynamic-update-slice_fusion.18
  397.4 1.8 copy-done.11
  (230 shorter events, 62.8 us)
Async XLA Ops:
  1.7 15.2 %collective-permute-start.1 = (f32[192,768]{1,0:T(8,128)S(1)}, f32[192,768]{1,0:T(8,128)S(1)}, u32[]{:S(2)}, u32[]{:S(2)}) collective-permute-start(f32[192,768]{1,0:T(8,128)S(1)} %dynamic-slice_convert_fusion.4), channel_id=1, source_target_pairs={{0,1},{1,0},{2,3},{3,2},{4,5},{5,4},{6,7},{7,6},{8,9},{9,8},{10,11... | collective-permute-start | bytes 1769480 | tf_op jit(solution)/shard_map/ppermute | solution.py:372
  14.7 18.4 %collective-permute-start.3 = (f32[512,384]{1,0:T(8,128)}, f32[512,384]{1,0:T(8,128)S(1)}, u32[]{:S(2)}, u32[]{:S(2)}) collective-permute-start(f32[512,384]{1,0:T(8,128)} %get-tuple-element.45.att_mine_ref), channel_id=1, source_target_pairs={{0,1},{1,0},{2,3},{3,2},{4,5},{5,4},{6,7},{7,6},{8,9},{9,8},{10,11... | collective-permute-start | bytes 2359304 | tf_op jit(solution)/shard_map/ppermute | solution.py:372
  16.8 14.7 %collective-permute-start.2 = (f32[192,768]{1,0:T(8,128)S(1)}, f32[192,768]{1,0:T(8,128)S(1)}, u32[]{:S(2)}, u32[]{:S(2)}) collective-permute-start(f32[192,768]{1,0:T(8,128)S(1)} %collective-permute-done.1), channel_id=1, source_target_pairs={{0,2},{2,0},{4,6},{6,4},{8,10},{10,8},{12,14},{14,12},{16,18},{18,... | collective-permute-start | bytes 1769480 | tf_op jit(solution)/shard_map/ppermute | solution.py:376
  18.5 10.7 %copy-start.35 = (f32[768]{0:T(1024)S(1)}, f32[768]{0:T(1024)}, u32[]{:S(2)}) copy-start(f32[768]{0:T(1024)} %param.23) | copy-start | bytes 9220
  18.5 11.3 %copy-start.31 = (f32[1536]{0:T(1024)S(1)}, f32[1536]{0:T(1024)}, u32[]{:S(2)}) copy-start(f32[1536]{0:T(1024)} %param.26) | copy-start | bytes 18436
  18.5 11.9 %copy-start.36 = (f32[768]{0:T(1024)S(1)}, f32[768]{0:T(1024)}, u32[]{:S(2)}) copy-start(f32[768]{0:T(1024)} %param.22) | copy-start | bytes 9220
  18.5 12.5 %copy-start.37 = (f32[768]{0:T(1024)S(1)}, f32[768]{0:T(1024)}, u32[]{:S(2)}) copy-start(f32[768]{0:T(1024)} %param.24) | copy-start | bytes 9220
  27.0 27.1 %collective-permute-start = (f32[512,384]{1,0:T(8,128)}, f32[512,384]{1,0:T(8,128)}, u32[]{:S(2)}, u32[]{:S(2)}) collective-permute-start(f32[512,384]{1,0:T(8,128)} %get-tuple-element.46.att_mine_ref), channel_id=1, source_target_pairs={{0,1},{1,0},{2,3},{3,2},{4,5},{5,4},{6,7},{7,6},{8,9},{9,8},{10,11... | collective-permute-start | bytes 2359304 | tf_op jit(solution)/shard_map/ppermute | solution.py:372
  48.9 36.4 %collective-permute-start.6 = (f32[512,768]{1,0:T(8,128)}, f32[512,768]{1,0:T(8,128)S(1)}, u32[]{:S(2)}, u32[]{:S(2)}) collective-permute-start(f32[512,768]{1,0:T(8,128)} %get-tuple-element.51), channel_id=1, source_target_pairs={{0,1},{1,0},{2,3},{3,2},{4,5},{5,4},{6,7},{7,6},{8,9},{9,8},{10,11... | collective-permute-start | bytes 4718600 | tf_op jit(solution)/shard_map/ppermute | solution.py:372
  50.7 65.4 %collective-permute-start.4 = (f32[512,768]{1,0:T(8,128)}, f32[512,768]{1,0:T(8,128)S(1)}, u32[]{:S(2)}, u32[]{:S(2)}) collective-permute-start(f32[512,768]{1,0:T(8,128)} %get-tuple-element.49), channel_id=1, source_target_pairs={{0,1},{1,0},{2,3},{3,2},{4,5},{5,4},{6,7},{7,6},{8,9},{9,8},{10,11... | collective-permute-start | bytes 4718600 | tf_op jit(solution)/shard_map/ppermute | solution.py:372
  72.0 6.6 %copy-start.17 = (bf16[512,1536]{1,0:T(8,128)(2,1)S(1)}, bf16[512,1536]{1,0:T(8,128)(2,1)}, u32[]{:S(2)}) copy-start(bf16[512,1536]{1,0:T(8,128)(2,1)} %get-tuple-element.73) | copy-start | bytes 4718596
  72.0 6.6 %copy-start.27 = (bf16[512,768]{1,0:T(8,128)(2,1)S(1)}, bf16[512,768]{1,0:T(8,128)(2,1)}, u32[]{:S(2)}) copy-start(bf16[512,768]{1,0:T(8,128)(2,1)} %get-tuple-element.72) | copy-start | bytes 2359300
  75.1 62.5 %collective-permute-start.36 = (f32[768,768]{1,0:T(8,128)}, f32[768,768]{1,0:T(8,128)}, u32[]{:S(2)}, u32[]{:S(2)}) collective-permute-start(f32[768,768]{1,0:T(8,128)} %constant_dynamic-slice_fusion.2), channel_id=1, source_target_pairs={{0,2},{2,0},{4,6},{6,4},{8,10},{10,8},{12,14},{14,12},{16,18},{18,... | collective-permute-start | bytes 7077896 | tf_op jit(solution)/shard_map/ppermute | solution.py:376
  84.5 58.2 %collective-permute-start.29 = (f32[384,1536]{1,0:T(8,128)}, f32[384,1536]{1,0:T(8,128)}, u32[]{:S(2)}, u32[]{:S(2)}) collective-permute-start(f32[384,1536]{1,0:T(8,128)} %constant_dynamic-slice_fusion.5), channel_id=1, source_target_pairs={{0,2},{2,0},{4,6},{6,4},{8,10},{10,8},{12,14},{14,12},{16,18},{18,... | collective-permute-start | bytes 7077896 | tf_op jit(solution)/shard_map/ppermute | solution.py:376
  86.5 29.8 %copy-start.34 = (f32[768]{0:T(1024)S(1)}, f32[768]{0:T(1024)}, u32[]{:S(2)}) copy-start(f32[768]{0:T(1024)} %param.28) | copy-start | bytes 9220
  91.8 58.1 %collective-permute-start.7 = (f32[512,768]{1,0:T(8,128)}, f32[512,768]{1,0:T(8,128)}, u32[]{:S(2)}, u32[]{:S(2)}) collective-permute-start(f32[512,768]{1,0:T(8,128)} %get-tuple-element.52.grad_middle_ref), channel_id=1, source_target_pairs={{0,1},{1,0},{2,3},{3,2},{4,5},{5,4},{6,7},{7,6},{8,9},{9,8},{10,11... | collective-permute-start | bytes 4718600 | tf_op jit(solution)/shard_map/ppermute | solution.py:372
  118.0 19.7 %slice-start = ((s8[4718592]{0:T(1024)(128)(4,1)}), s8[4194304]{0:T(1024)(128)(4,1)S(1)}, s32[]{:S(2)}) async-start(s8[4718592]{0:T(1024)(128)(4,1)} %bitcast.40), calls=%async_computation | async-start | bytes 8388608
  119.5 205.7 %collective-permute-start.5 = (f32[512,768]{1,0:T(8,128)}, f32[512,768]{1,0:T(8,128)}, u32[]{:S(2)}, u32[]{:S(2)}) collective-permute-start(f32[512,768]{1,0:T(8,128)} %get-tuple-element.92), channel_id=1, source_target_pairs={{0,1},{1,0},{2,3},{3,2},{4,5},{5,4},{6,7},{7,6},{8,9},{9,8},{10,11... | collective-permute-start | bytes 4718600 | tf_op jit(solution)/shard_map/ppermute | solution.py:372
  121.2 11.4 %copy-start.3 = (bf16[512,768]{1,0:T(8,128)(2,1)S(1)}, bf16[512,768]{1,0:T(8,128)(2,1)}, u32[]{:S(2)}) copy-start(bf16[512,768]{1,0:T(8,128)(2,1)} %get-tuple-element.66) | copy-start | bytes 2359300
  121.2 16.4 %slice-start.1 = ((s8[4718592]{0:T(1024)(128)(4,1)}), s8[524288]{0:T(1024)(128)(4,1)S(1)}, s32[]{:S(2)}) async-start(s8[4718592]{0:T(1024)(128)(4,1)} %bitcast.40), calls=%async_computation.1 | async-start | bytes 1048576
  141.0 36.4 %collective-permute-start.37 = (f32[384,768]{1,0:T(8,128)}, f32[384,768]{1,0:T(8,128)}, u32[]{:S(2)}, u32[]{:S(2)}) collective-permute-start(f32[384,768]{1,0:T(8,128)} %constant_dynamic-slice_fusion.1), channel_id=1, source_target_pairs={{0,4},{2,6},{4,0},{6,2},{8,12},{10,14},{12,8},{14,10},{16,20},{18,... | collective-permute-start | bytes 3538952 | tf_op jit(solution)/shard_map/ppermute | solution.py:376
  145.9 5.9 %copy-start.5 = (f32[512,768]{1,0:T(8,128)S(1)}, f32[512,768]{1,0:T(8,128)}, u32[]{:S(2)}) copy-start(f32[512,768]{1,0:T(8,128)} %get-tuple-element.52.grad_middle_ref) | copy-start | bytes 4718596
  145.9 5.9 %copy-start.25 = (f32[512,384]{1,0:T(8,128)S(1)}, f32[512,384]{1,0:T(8,128)}, u32[]{:S(2)}) copy-start(f32[512,384]{1,0:T(8,128)} %get-tuple-element.45.att_mine_ref) | copy-start | bytes 2359300
  145.9 41.3 %collective-permute-start.30 = (f32[192,1536]{1,0:T(8,128)}, f32[192,1536]{1,0:T(8,128)}, u32[]{:S(2)}, u32[]{:S(2)}) collective-permute-start(f32[192,1536]{1,0:T(8,128)} %constant_dynamic-slice_fusion.4), channel_id=1, source_target_pairs={{0,4},{2,6},{4,0},{6,2},{8,12},{10,14},{12,8},{14,10},{16,20},{18,... | collective-permute-start | bytes 3538952 | tf_op jit(solution)/shard_map/ppermute | solution.py:376
  152.3 8.3 %copy-start.9 = (f32[384,768]{1,0:T(8,128)}, f32[384,768]{1,0:T(8,128)S(1)}, u32[]{:S(2)}) copy-start(f32[384,768]{1,0:T(8,128)S(1)} %convolution_add_fusion.2) | copy-start | bytes 3538948
  153.3 26.9 %collective-permute-start.22 = (f32[192,768]{1,0:T(8,128)}, f32[192,768]{1,0:T(8,128)}, u32[]{:S(2)}, u32[]{:S(2)}) collective-permute-start(f32[192,768]{1,0:T(8,128)} %constant_dynamic-slice_fusion.8), channel_id=1, source_target_pairs={{0,2},{2,0},{4,6},{6,4},{8,10},{10,8},{12,14},{14,12},{16,18},{18,... | collective-permute-start | bytes 1769480 | tf_op jit(solution)/shard_map/ppermute | solution.py:376
  160.7 11.2 %copy-start.2 = (bf16[512,768]{1,0:T(8,128)(2,1)S(1)}, bf16[512,768]{1,0:T(8,128)(2,1)}, u32[]{:S(2)}) copy-start(bf16[512,768]{1,0:T(8,128)(2,1)} %get-tuple-element.68) | copy-start | bytes 2359300
  175.9 34.1 %collective-permute-start.15 = (f32[1152,384]{1,0:T(8,128)S(1)}, f32[1152,384]{1,0:T(8,128)S(1)}, u32[]{:S(2)}, u32[]{:S(2)}) collective-permute-start(f32[1152,384]{1,0:T(8,128)S(1)} %constant_dynamic-slice_fusion.11), channel_id=1, source_target_pairs={{0,2},{2,0},{4,6},{6,4},{8,10},{10,8},{12,14},{14,12},{16,18},{18,... | collective-permute-start | bytes 5308424 | tf_op jit(solution)/shard_map/ppermute | solution.py:376
  177.5 63.0 %collective-permute-start.8 = (f32[512,768]{1,0:T(8,128)S(1)}, f32[512,768]{1,0:T(8,128)}, u32[]{:S(2)}, u32[]{:S(2)}) collective-permute-start(f32[512,768]{1,0:T(8,128)S(1)} %copy-done.38), channel_id=1, source_target_pairs={{0,1},{1,0},{2,3},{3,2},{4,5},{5,4},{6,7},{7,6},{8,9},{9,8},{10,11... | collective-permute-start | bytes 4718600 | tf_op jit(solution)/shard_map/ppermute | solution.py:372
  180.2 18.0 %collective-permute-start.38 = (f32[192,768]{1,0:T(8,128)S(1)}, f32[192,768]{1,0:T(8,128)S(1)}, u32[]{:S(2)}, u32[]{:S(2)}) collective-permute-start(f32[192,768]{1,0:T(8,128)S(1)} %constant_dynamic-slice_fusion), channel_id=1, source_target_pairs={{0,8},{2,10},{4,12},{6,14},{8,0},{10,2},{12,4},{14,6},{16,24},{18,... | collective-permute-start | bytes 1769480 | tf_op jit(solution)/shard_map/ppermute | solution.py:376
  187.2 9.4 %collective-permute-start.23 = (f32[96,768]{1,0:T(8,128)S(1)}, f32[96,768]{1,0:T(8,128)S(1)}, u32[]{:S(2)}, u32[]{:S(2)}) collective-permute-start(f32[96,768]{1,0:T(8,128)S(1)} %constant_dynamic-slice_fusion.7), channel_id=1, source_target_pairs={{0,4},{2,6},{4,0},{6,2},{8,12},{10,14},{12,8},{14,10},{16,20},{18,... | collective-permute-start | bytes 884744 | tf_op jit(solution)/shard_map/ppermute | solution.py:376
  196.6 13.8 %collective-permute-start.31 = (f32[96,1536]{1,0:T(8,128)S(1)}, f32[96,1536]{1,0:T(8,128)S(1)}, u32[]{:S(2)}, u32[]{:S(2)}) collective-permute-start(f32[96,1536]{1,0:T(8,128)S(1)} %constant_dynamic-slice_fusion.3), channel_id=1, source_target_pairs={{0,8},{2,10},{4,12},{6,14},{8,0},{10,2},{12,4},{14,6},{16,24},{18,... | collective-permute-start | bytes 1769480 | tf_op jit(solution)/shard_map/ppermute | solution.py:376
  198.3 9.2 %collective-permute-start.24 = (f32[48,768]{1,0:T(8,128)S(1)}, f32[48,768]{1,0:T(8,128)S(1)}, u32[]{:S(2)}, u32[]{:S(2)}) collective-permute-start(f32[48,768]{1,0:T(8,128)S(1)} %constant_dynamic-slice_fusion.6), channel_id=1, source_target_pairs={{0,8},{2,10},{4,12},{6,14},{8,0},{10,2},{12,4},{14,6},{16,24},{18,... | collective-permute-start | bytes 442376 | tf_op jit(solution)/shard_map/ppermute | solution.py:376
  207.4 28.5 %collective-permute-start.39 = (f32[192,768]{1,0:T(8,128)S(1)}, f32[192,768]{1,0:T(8,128)S(1)}, u32[]{:S(2)}, u32[]{:S(2)}) collective-permute-start(f32[192,768]{1,0:T(8,128)S(1)} %dynamic-slice_add_fusion.6), channel_id=1, source_target_pairs={{0,16},{2,18},{4,20},{6,22},{8,24},{10,26},{12,28},{14,30},{16,0},... | collective-permute-start | bytes 1769480 | tf_op jit(solution)/shard_map/ppermute | solution.py:376
  210.0 25.2 %collective-permute-start.25 = (f32[48,768]{1,0:T(8,128)S(1)}, f32[48,768]{1,0:T(8,128)S(1)}, u32[]{:S(2)}, u32[]{:S(2)}) collective-permute-start(f32[48,768]{1,0:T(8,128)S(1)} %dynamic-slice_add_fusion.11), channel_id=1, source_target_pairs={{0,16},{2,18},{4,20},{6,22},{8,24},{10,26},{12,28},{14,30},{16,0},... | collective-permute-start | bytes 442376 | tf_op jit(solution)/shard_map/ppermute | solution.py:376
  210.4 36.0 %collective-permute-start.16 = (f32[576,384]{1,0:T(8,128)S(1)}, f32[576,384]{1,0:T(8,128)S(1)}, u32[]{:S(2)}, u32[]{:S(2)}) collective-permute-start(f32[576,384]{1,0:T(8,128)S(1)} %constant_dynamic-slice_fusion.10), channel_id=1, source_target_pairs={{0,4},{2,6},{4,0},{6,2},{8,12},{10,14},{12,8},{14,10},{16,20},{18,... | collective-permute-start | bytes 2654216 | tf_op jit(solution)/shard_map/ppermute | solution.py:376
  235.2 20.1 %collective-permute-start.32 = (f32[96,1536]{1,0:T(8,128)S(1)}, f32[96,1536]{1,0:T(8,128)S(1)}, u32[]{:S(2)}, u32[]{:S(2)}) collective-permute-start(f32[96,1536]{1,0:T(8,128)S(1)} %dynamic-slice_add_fusion.7), channel_id=1, source_target_pairs={{0,16},{2,18},{4,20},{6,22},{8,24},{10,26},{12,28},{14,30},{16,0},... | collective-permute-start | bytes 1769480 | tf_op jit(solution)/shard_map/ppermute | solution.py:376
  235.9 56.8 %collective-permute-start.26 = (f32[48,768]{1,0:T(8,128)}, f32[48,768]{1,0:T(8,128)S(1)}, u32[]{:S(2)}, u32[]{:S(2)}) collective-permute-start(f32[48,768]{1,0:T(8,128)} %get-tuple-element.88), channel_id=1, source_target_pairs={{0,8},{2,10},{4,12},{6,14},{8,0},{10,2},{12,4},{14,6},{16,24},{18,... | collective-permute-start | bytes 442376 | tf_op jit(solution)/shard_map/ppermute | solution.py:376
  240.5 24.0 %collective-permute-start.40 = (f32[192,768]{1,0:T(8,128)S(1)}, f32[192,768]{1,0:T(8,128)}, u32[]{:S(2)}, u32[]{:S(2)}) collective-permute-start(f32[192,768]{1,0:T(8,128)S(1)} %get-tuple-element.84), channel_id=1, source_target_pairs={{0,8},{2,10},{4,12},{6,14},{8,0},{10,2},{12,4},{14,6},{16,24},{18,... | collective-permute-start | bytes 1769480 | tf_op jit(solution)/shard_map/ppermute | solution.py:376
  246.4 18.0 %collective-permute-start.10 = (f32[6,768]{1,0:T(8,128)S(1)}, f32[6,768]{1,0:T(8,128)S(1)}, u32[]{:S(2)}, u32[]{:S(2)}) collective-permute-start(f32[6,768]{1,0:T(8,128)S(1)} %pad_maximum_fusion.1), channel_id=1, source_target_pairs={{0,1},{1,0},{2,3},{3,2},{4,5},{5,4},{6,7},{7,6},{8,9},{9,8},{10,11... | collective-permute-start | bytes 55304 | tf_op jit(solution)/shard_map/ppermute | solution.py:372
  255.3 14.7 %collective-permute-start.17 = (f32[288,384]{1,0:T(8,128)S(1)}, f32[288,384]{1,0:T(8,128)S(1)}, u32[]{:S(2)}, u32[]{:S(2)}) collective-permute-start(f32[288,384]{1,0:T(8,128)S(1)} %constant_dynamic-slice_fusion.9), channel_id=1, source_target_pairs={{0,8},{2,10},{4,12},{6,14},{8,0},{10,2},{12,4},{14,6},{16,24},{18,... | collective-permute-start | bytes 1327112 | tf_op jit(solution)/shard_map/ppermute | solution.py:376
  264.4 23.1 %collective-permute-start.33 = (f32[96,1536]{1,0:T(8,128)S(1)}, f32[96,1536]{1,0:T(8,128)S(1)}, u32[]{:S(2)}, u32[]{:S(2)}) collective-permute-start(f32[96,1536]{1,0:T(8,128)S(1)} %get-tuple-element.86), channel_id=1, source_target_pairs={{0,8},{2,10},{4,12},{6,14},{8,0},{10,2},{12,4},{14,6},{16,24},{18,... | collective-permute-start | bytes 1769480 | tf_op jit(solution)/shard_map/ppermute | solution.py:376
  265.6 27.0 %copy-start.29 = (f32[1,1536]{1,0:T(1,128)S(1)}, f32[1,1536]{1,0:T(1,128)}, u32[]{:S(2)}) copy-start(f32[1,1536]{1,0:T(1,128)} %add.254) | copy-start | bytes 18436
  265.6 27.0 %copy-start.30 = (f32[1,1536]{1,0:T(1,128)S(1)}, f32[1,1536]{1,0:T(1,128)}, u32[]{:S(2)}) copy-start(f32[1,1536]{1,0:T(1,128)} %pad.28) | copy-start | bytes 18436
  265.6 48.1 %collective-permute-start.41 = (f32[384,768]{1,0:T(8,128)S(1)}, f32[384,768]{1,0:T(8,128)}, u32[]{:S(2)}, u32[]{:S(2)}) collective-permute-start(f32[384,768]{1,0:T(8,128)S(1)} %constant_dynamic-update-slice_fusion.4), channel_id=1, source_target_pairs={{0,4},{2,6},{4,0},{6,2},{8,12},{10,14},{12,8},{14,10},{16,20},{18,... | collective-permute-start | bytes 3538952 | tf_op jit(solution)/shard_map/ppermute | solution.py:376
  270.1 39.1 %collective-permute-start.18 = (f32[288,384]{1,0:T(8,128)S(1)}, f32[288,384]{1,0:T(8,128)S(1)}, u32[]{:S(2)}, u32[]{:S(2)}) collective-permute-start(f32[288,384]{1,0:T(8,128)S(1)} %dynamic-slice_add_fusion.9), channel_id=1, source_target_pairs={{0,16},{2,18},{4,20},{6,22},{8,24},{10,26},{12,28},{14,30},{16,0},... | collective-permute-start | bytes 1327112 | tf_op jit(solution)/shard_map/ppermute | solution.py:376
  288.4 34.2 %collective-permute-start.34 = (f32[192,1536]{1,0:T(8,128)}, f32[192,1536]{1,0:T(8,128)}, u32[]{:S(2)}, u32[]{:S(2)}) collective-permute-start(f32[192,1536]{1,0:T(8,128)} %constant_dynamic-update-slice_fusion.10), channel_id=1, source_target_pairs={{0,4},{2,6},{4,0},{6,2},{8,12},{10,14},{12,8},{14,10},{16,20},{18,... | collective-permute-start | bytes 3538952 | tf_op jit(solution)/shard_map/ppermute | solution.py:376
  292.7 11.5 %collective-permute-start.11 = (f32[8,1536]{1,0:T(8,128)S(1)}, f32[8,1536]{1,0:T(8,128)S(1)}, u32[]{:S(2)}, u32[]{:S(2)}) collective-permute-start(f32[8,1536]{1,0:T(8,128)S(1)} %concatenate.18), channel_id=1, source_target_pairs={{0,2},{2,0},{4,6},{6,4},{8,10},{10,8},{12,14},{14,12},{16,18},{18,... | collective-permute-start | bytes 147464 | tf_op jit(solution)/shard_map/ppermute | solution.py:376
  303.3 6.0 %copy-start.23 = (f32[96,768]{1,0:T(8,128)}, f32[96,768]{1,0:T(8,128)S(1)}, u32[]{:S(2)}) copy-start(f32[96,768]{1,0:T(8,128)S(1)} %constant_dynamic-update-slice_fusion.16) | copy-start | bytes 884740
  304.2 77.1 %collective-permute-start.9 = (f32[512,768]{1,0:T(8,128)}, f32[512,768]{1,0:T(8,128)}, u32[]{:S(2)}, u32[]{:S(2)}) collective-permute-start(f32[512,768]{1,0:T(8,128)} %get-tuple-element.59), channel_id=1, source_target_pairs={{0,1},{1,0},{2,3},{3,2},{4,5},{5,4},{6,7},{7,6},{8,9},{9,8},{10,11... | collective-permute-start | bytes 4718600 | tf_op jit(solution)/shard_map/ppermute | solution.py:372
  309.3 8.8 %collective-permute-start.19 = (f32[288,384]{1,0:T(8,128)S(1)}, f32[288,384]{1,0:T(8,128)S(1)}, u32[]{:S(2)}, u32[]{:S(2)}) collective-permute-start(f32[288,384]{1,0:T(8,128)S(1)} %get-tuple-element.90), channel_id=1, source_target_pairs={{0,8},{2,10},{4,12},{6,14},{8,0},{10,2},{12,4},{14,6},{16,24},{18,... | collective-permute-start | bytes 1327112 | tf_op jit(solution)/shard_map/ppermute | solution.py:376
  313.7 12.8 %collective-permute-start.12 = (f32[8,1536]{1,0:T(8,128)S(1)}, f32[8,1536]{1,0:T(8,128)S(1)}, u32[]{:S(2)}, u32[]{:S(2)}) collective-permute-start(f32[8,1536]{1,0:T(8,128)S(1)} %add.256), channel_id=1, source_target_pairs={{0,4},{2,6},{4,0},{6,2},{8,12},{10,14},{12,8},{14,10},{16,20},{18,... | collective-permute-start | bytes 147464 | tf_op jit(solution)/shard_map/ppermute | solution.py:376
  313.7 11.5 %copy-start.24 = (f32[96,768]{1,0:T(8,128)S(1)}, f32[96,768]{1,0:T(8,128)}, u32[]{:S(2)}) copy-start(f32[96,768]{1,0:T(8,128)} %copy-done.23) | copy-start | bytes 884740
  318.1 70.7 %collective-permute-start.42 = (f32[768,768]{1,0:T(8,128)S(1)}, f32[768,768]{1,0:T(8,128)}, u32[]{:S(2)}, u32[]{:S(2)}) collective-permute-start(f32[768,768]{1,0:T(8,128)S(1)} %constant_dynamic-update-slice_fusion.2), channel_id=1, source_target_pairs={{0,2},{2,0},{4,6},{6,4},{8,10},{10,8},{12,14},{14,12},{16,18},{18,... | collective-permute-start | bytes 7077896 | tf_op jit(solution)/shard_map/ppermute | solution.py:376
  322.5 20.0 %copy-start.13 = (f32[1024,768]{1,0:T(8,128)S(1)}, f32[1024,768]{1,0:T(8,128)}, u32[]{:S(2)}) copy-start(f32[1024,768]{1,0:T(8,128)} %copy-done.12) | copy-start | bytes 9437188
  322.6 41.6 %collective-permute-start.20 = (f32[576,384]{1,0:T(8,128)S(1)}, f32[576,384]{1,0:T(8,128)S(1)}, u32[]{:S(2)}, u32[]{:S(2)}) collective-permute-start(f32[576,384]{1,0:T(8,128)S(1)} %constant_dynamic-update-slice_fusion.22), channel_id=1, source_target_pairs={{0,4},{2,6},{4,0},{6,2},{8,12},{10,14},{12,8},{14,10},{16,20},{18,... | collective-permute-start | bytes 2654216 | tf_op jit(solution)/shard_map/ppermute | solution.py:376
  325.2 22.8 %collective-permute-start.27 = (f32[96,768]{1,0:T(8,128)S(1)}, f32[96,768]{1,0:T(8,128)S(1)}, u32[]{:S(2)}, u32[]{:S(2)}) collective-permute-start(f32[96,768]{1,0:T(8,128)S(1)} %copy-done.24), channel_id=1, source_target_pairs={{0,4},{2,6},{4,0},{6,2},{8,12},{10,14},{12,8},{14,10},{16,20},{18,... | collective-permute-start | bytes 884744 | tf_op jit(solution)/shard_map/ppermute | solution.py:376
  326.5 64.3 %collective-permute-start.35 = (f32[384,1536]{1,0:T(8,128)}, f32[384,1536]{1,0:T(8,128)}, u32[]{:S(2)}, u32[]{:S(2)}) collective-permute-start(f32[384,1536]{1,0:T(8,128)} %constant_dynamic-update-slice_fusion.8), channel_id=1, source_target_pairs={{0,2},{2,0},{4,6},{6,4},{8,10},{10,8},{12,14},{14,12},{16,18},{18,... | collective-permute-start | bytes 7077896 | tf_op jit(solution)/shard_map/ppermute | solution.py:376
  344.0 19.1 %copy-start.14 = (f32[1024,768]{1,0:T(8,128)}, f32[1024,768]{1,0:T(8,128)S(1)}, u32[]{:S(2)}) copy-start(f32[1024,768]{1,0:T(8,128)S(1)} %constant_dynamic-update-slice_fusion.26) | copy-start | bytes 9437188
  346.7 17.4 %copy-start.15 = (f32[1024,768]{1,0:T(8,128)}, f32[1024,768]{1,0:T(8,128)S(1)}, u32[]{:S(2)}) copy-start(f32[1024,768]{1,0:T(8,128)S(1)} %constant_dynamic-update-slice_fusion.25) | copy-start | bytes 9437188
  348.0 3.2 collective-permute-start.13
  351.2 29.2 %collective-permute-start.28 = (f32[192,768]{1,0:T(8,128)S(1)}, f32[192,768]{1,0:T(8,128)S(1)}, u32[]{:S(2)}, u32[]{:S(2)}) collective-permute-start(f32[192,768]{1,0:T(8,128)S(1)} %constant_dynamic-update-slice_fusion.14), channel_id=1, source_target_pairs={{0,2},{2,0},{4,6},{6,4},{8,10},{10,8},{12,14},{14,12},{16,18},{18,... | collective-permute-start | bytes 1769480 | tf_op jit(solution)/shard_map/ppermute | solution.py:376
  364.1 9.5 %collective-permute-start.14 = (f32[8,1536]{1,0:T(8,128)S(1)}, f32[8,1536]{1,0:T(8,128)S(1)}, u32[]{:S(2)}, u32[]{:S(2)}) collective-permute-start(f32[8,1536]{1,0:T(8,128)S(1)} %add.258), channel_id=1, source_target_pairs={{0,16},{2,18},{4,20},{6,22},{8,24},{10,26},{12,28},{14,30},{16,0},... | collective-permute-start | bytes 147464 | tf_op jit(solution)/shard_map/ppermute | solution.py:376
  373.6 20.8 %collective-permute-start.21 = (f32[1152,384]{1,0:T(8,128)}, f32[1152,384]{1,0:T(8,128)}, u32[]{:S(2)}, u32[]{:S(2)}) collective-permute-start(f32[1152,384]{1,0:T(8,128)} %constant_dynamic-update-slice_fusion.20), channel_id=1, source_target_pairs={{0,2},{2,0},{4,6},{6,4},{8,10},{10,8},{12,14},{14,12},{16,18},{18,... | collective-permute-start | bytes 5308424 | tf_op jit(solution)/shard_map/ppermute | solution.py:376
  (23 other events, 60.4 us)
